TPU v7x, 32 devices: a whole 2x2x4 slice. The times are simulated.
32 devices in a mesh: row: 8 (over y, x, core), col: 4 (over z).
Axes of the slice: x: 2, y: 2, z: 4, core: 2. Of those that a mesh axis runs over, the one named last changes fastest.
Arguments:
- item_features: bfloat16 [16384, 256], P(('row', 'col')), may hold values from -6 to 6
- self_weight: bfloat16 [256, 256], replicated, may hold values from -0.375 to 0.375
- neighbor_weight: bfloat16 [256, 256], replicated, may hold values from -0.375 to 0.375
- layer_bias: float32 [256], replicated, may hold values from -3 to 3
- norm_gain: float32 [256], replicated, may hold values from 0.5 to 1.5
- blocks: bfloat16 [8, 4, 256, 128, 128], P('row', 'col'), may hold values from 0 to 0.0625
- block_rows: int32 [8, 4, 256], P('row', 'col'), may hold values from 0 to 15, as said below
- block_cols: int32 [8, 4, 256], P('row', 'col'), may hold values from 0 to 31, as said below
- counts: int32 [8, 4], P('row', 'col'), may hold values from 1 to 256, as said below
- queries: bfloat16 [512, 256], P(('row', 'col')), may hold values from -6 to 6
- candidates: int32 [512, 64], P(('row', 'col')), may hold values from 0 to 16383, as said below
- positions: int32 [512, 64], P(('row', 'col')), may hold values from 0 to 63, each once within a row
- position_table: float32 [64, 128], replicated, may hold values from -6 to 6
- tower_weight: float32 [128], replicated, may hold values from -0.5 to 0.5
- score_cotangent: bfloat16 [512, 64], P(('row', 'col')), may hold values from -6 to 6
Outputs:
- hidden: bfloat16 [16384, 256], P(('row', 'col'))
- scores: float32 [512, 64], P(('row', 'col'))
- item_grads: float32 [16384, 256], P(('row', 'col'))
Inputs may be any that keep to these rules, and one draw needn't show every extreme that they name: Slots s >= counts[r, c] are not part of A. In every draw all devices of some row have 256 live slots. `block_rows`: the live slots of one device name distinct pairs of block row and block column. `block_cols`: the live slots of one device name distinct pairs of block row and block column. The candidates of requests of piece p (rows p * 16 to (p + 1) * 16 - 1) are items of column set p % 4; an item may appear several times.
All inputs are finite; a program needn't handle non-finite values.
Results may differ from a plain program's by a relative error of at most 0.04.
Values may be sent and summed in bfloat16 or wider, within the bound.
A program may use at most 128 MiB of HBM per device.

v0:
```python
import math

import jax
import jax.numpy as jnp
from jax import lax
from jax.sharding import PartitionSpec as P

norm_eps = 1e-05


def normalize(preact, norm_gain):
    active = jax.nn.silu(preact)
    return (
        norm_gain * active * lax.rsqrt(jnp.mean(active * active, axis=-1, keepdims=True) + norm_eps)
    )


def block_products(
    tile_set, targets, sources, live_count, first_block, seg_count, source, transpose
):
    slot_total = tile_set.shape[0]
    block_size = tile_set.shape[1]
    feature_width = source.shape[-1]
    group_size = math.gcd(64, slot_total)
    slot_index = jnp.arange(slot_total, dtype=jnp.int32)
    is_live = (
        (slot_index < live_count) & (targets >= first_block) & (targets < first_block + seg_count)
    )
    ordering = jnp.argsort(jnp.where(is_live, slot_index, slot_total + slot_index))
    live_total = jnp.sum(is_live.astype(jnp.int32))
    shaped = source.reshape(-1, block_size, feature_width)

    def add_group(group_index, summed):
        picked = lax.dynamic_slice_in_dim(ordering, group_index * group_size, group_size)
        is_valid = group_index * group_size + jnp.arange(group_size) < live_total
        tile_group = tile_set[picked]
        source_rows = shaped[sources[picked]]
        if transpose:
            product = jnp.einsum(
                "gij,gid->gjd", tile_group, source_rows, preferred_element_type=jnp.float32
            )
        else:
            product = jnp.einsum(
                "gij,gjd->gid", tile_group, source_rows, preferred_element_type=jnp.float32
            )
        segment = jnp.where(is_valid, targets[picked], seg_count)
        return summed.at[segment].add(product, mode="drop")

    group_total = (live_total + group_size - 1) // group_size
    summed = lax.fori_loop(
        0, group_total, add_group, jnp.zeros((seg_count, block_size, feature_width), jnp.float32)
    )
    return summed.reshape(seg_count * block_size, feature_width)


def body(
    item_features,
    self_weight,
    neighbor_weight,
    layer_bias,
    norm_gain,
    blocks,
    block_rows,
    block_cols,
    counts,
    queries,
    candidates,
    positions,
    position_table,
    tower_weight,
    score_cotangent,
):
    rows_dev, feature_width = item_features.shape
    tile_set = blocks[0, 0]
    tile_rows = block_rows[0, 0]
    tile_cols = block_cols[0, 0]
    live_count = counts[0, 0]
    block_size = tile_set.shape[1]
    column_items, all_queries, all_ids, all_cotangent = (
        lax.all_gather(item_features, "row", axis=0, tiled=True),
        lax.all_gather(queries, "row", axis=0, tiled=True),
        lax.all_gather(candidates, "row", axis=0, tiled=True),
        lax.all_gather(score_cotangent, "row", axis=0, tiled=True),
    )
    aggregate = lax.psum_scatter(
        block_products(
            tile_set,
            tile_rows,
            tile_cols,
            live_count,
            jnp.int32(0) // block_size,
            lax.axis_size("col") * rows_dev // block_size,
            column_items,
            False,
        ).astype(jnp.bfloat16),
        "col",
        scatter_dimension=0,
        tiled=True,
    )
    preact = jnp.dot(item_features, self_weight, preferred_element_type=jnp.float32)
    preact = (
        preact
        + jnp.dot(aggregate, neighbor_weight, preferred_element_type=jnp.float32)
        + layer_bias
    )
    normed, pullback = jax.vjp(lambda value: normalize(value, norm_gain), preact)
    hidden = normed.astype(jnp.bfloat16)
    score_scale = feature_width ** (-0.5)
    col_count = lax.axis_size("col")
    my_piece = lax.axis_index("row") * col_count + lax.axis_index("col")
    is_mine = all_ids // rows_dev == my_piece
    local_rows = all_ids % rows_dev
    target = candidates // rows_dev // col_count * rows_dev + candidates % rows_dev
    piece = lax.all_gather(hidden, "row", axis=0, tiled=True)
    offset = jnp.int32(0)
    row_count = piece.shape[0]
    score_table = jnp.einsum("qd,nd->qn", queries, piece, preferred_element_type=jnp.float32)
    inside = (target >= offset) & (target < offset + row_count)
    picked = jnp.take_along_axis(score_table, jnp.clip(target, 0, row_count - 1), axis=1)
    raw_scores = jnp.where(inside, picked, 0.0)
    tower_values = jnp.sum(jax.nn.relu(position_table) * tower_weight, axis=-1)
    position_hits = positions[..., None] == jnp.arange(tower_values.shape[0])
    scores = raw_scores * score_scale + jnp.sum(
        jnp.where(position_hits, tower_values, 0.0), axis=-1
    )
    gathered_requests = all_queries.shape[0]
    flat_index = jnp.where(
        is_mine,
        local_rows * gathered_requests + jnp.arange(gathered_requests)[:, None],
        rows_dev * gathered_requests,
    )
    weights = jnp.zeros((rows_dev * gathered_requests,), jnp.float32)
    weights = weights.at[flat_index.reshape(-1)].add(
        all_cotangent.astype(jnp.float32).reshape(-1), mode="drop"
    )
    weights = weights.reshape(rows_dev, gathered_requests)
    grad_hidden = (
        jnp.dot(weights, all_queries.astype(jnp.float32), precision=lax.Precision.HIGHEST)
        * score_scale
    )
    grad_preact = pullback(grad_hidden)[0]
    grad_rounded = grad_preact.astype(jnp.bfloat16)
    grad_self = jnp.einsum(
        "nd,ed->ne", grad_rounded, self_weight, preferred_element_type=jnp.float32
    )
    back_source = jnp.einsum(
        "nd,ed->ne", grad_rounded, neighbor_weight, preferred_element_type=jnp.float32
    ).astype(jnp.bfloat16)
    range_source = lax.all_gather(back_source, "col", axis=0, tiled=True)
    back_sum = lax.psum_scatter(
        block_products(
            tile_set,
            tile_cols,
            tile_rows,
            live_count,
            jnp.int32(0) // block_size,
            lax.axis_size("row") * rows_dev // block_size,
            range_source,
            True,
        ).astype(jnp.bfloat16),
        "row",
        scatter_dimension=0,
        tiled=True,
    ).astype(jnp.float32)
    return (hidden, scores, grad_self + back_sum)


def solution(mesh):
    in_specs = (
        P(("row", "col"), None),
        P(),
        P(),
        P(),
        P(),
        P("row", "col", None, None, None),
        P("row", "col", None),
        P("row", "col", None),
        P("row", "col"),
        P(("row", "col"), None),
        P(("row", "col"), None),
        P(("row", "col"), None),
        P(),
        P(),
        P(("row", "col"), None),
    )
    out_specs = (P(("row", "col"), None), P(("row", "col"), None), P(("row", "col"), None))
    return jax.shard_map(body, mesh=mesh, in_specs=in_specs, out_specs=out_specs, check_vma=False)
```

profile of v0, /device:TPU:0, one launch (start us, length us, event | category | flops | bytes accessed | tf_op | source)
XLA Modules:
  0.0 463.5 jit_solution(9591028152479299945)
XLA Ops:
  10.6 3.2 sort.31
  13.8 10.8 %all_gather.20 = s32[128,64]{1,0:T(8,128)S(1)} all-gather(s32[16,64]{1,0:T(8,128)} %param.29), channel_id=1, replica_groups=mesh['row'=8,'col'=4] {'row'}, dimensions={0}, use_global_device_ids=true | all-gather | bytes 36864 | tf_op jit(solution)/shard_map/all_gather | solution.py:82
  24.6 16.0 %all-gather.4.cloned.1.call-done = bf16[4096,256]{1,0:T(8,128)(2,1)} async-done(((bf16[512,256]{1,0:T(8,128)(2,1)}), bf16[4096,256]{1,0:T(8,128)(2,1)}) %all-gather.4.cloned.1.call-update) | async-done | bytes 2097168 | tf_op jit(solution)/shard_map/all_gather | solution.py:80
  40.8 130.2 %while.20 = (s32[]{:T(128)}, f32[16,128,256]{2,1,0:T(8,128)S(1)}, s32[]{:T(128)}, s32[]{:T(128)}, s32[256]{0:T(256)S(1)}, /*index=5*/s32[256]{0:T(256)}, bf16[25...) while((s32[]{:T(128)}, f32[16,128,256]{2,1,0:T(8,128)S(1)}, ...), condition=%wide.region_4.5_spmd, body=%wide.region_2.4_spmd.sunk | while | flops 538970880 | bytes 52445648 | solution.py:50
  42.4 4.4 gather_fusion.3
  46.8 5.5 %gather_fusion.1 = bf16[64,128,128]{2,1,0:T(8,128)(2,1)} fusion(bf16[256,128,128]{2,1,0:T(8,128)(2,1)} %get-tuple-element.308, s32[1024]{0:T(1024)S(1)} %pad_clamp_fusion.8), kind=kCustom, calls=%fused_computation.1.clone.1 | custom fusion | bytes 4194560 | tf_op jit(solution)/shard_map/while/body/gather | solution.py:36
  52.3 7.3 %fusion.59 = f32[64,128,256]{2,1,0:T(8,128)} fusion(bf16[64,128,128]{2,1,0:T(8,128)(2,1)} %gather_fusion.1, bf16[64,128,256]{2,1,0:T(8,128)(2,1)} %gather_fusion.3), kind=kOutput, calls=%fused_computation.95.clone.1 | convolution fusion | flops 536870912 | bytes 14680064 | tf_op jit(solution)/shard_map/while/body/gij,gjd->gid/dot_general | solution.py:43
  61.1 12.3 %scatter_fusion = f32[16,128,256]{2,1,0:T(8,128)S(1)} fusion(f32[16,128,256]{2,1,0:T(8,128)S(1)} %get-tuple-element.290, s32[64]{0:T(128)S(1)} %fusion.57, f32[64,128,256]{2,1,0:T(8,128)} %fusion.59), kind=kCustom, calls=%fused_computation.9.clone.1 | custom fusion | flops 2097152 | bytes 25166080 | tf_op jit(solution)/shard_map/while/body/scatter-add | solution.py:47
  75.0 4.4 gather_fusion.3
  79.3 5.5 %gather_fusion.1 = bf16[64,128,128]{2,1,0:T(8,128)(2,1)} fusion(bf16[256,128,128]{2,1,0:T(8,128)(2,1)} %get-tuple-element.308, s32[1024]{0:T(1024)S(1)} %pad_clamp_fusion.8), kind=kCustom, calls=%fused_computation.1.clone.1 | custom fusion | bytes 4194560 | tf_op jit(solution)/shard_map/while/body/gather | solution.py:36
  84.9 7.3 %fusion.59 = f32[64,128,256]{2,1,0:T(8,128)} fusion(bf16[64,128,128]{2,1,0:T(8,128)(2,1)} %gather_fusion.1, bf16[64,128,256]{2,1,0:T(8,128)(2,1)} %gather_fusion.3), kind=kOutput, calls=%fused_computation.95.clone.1 | convolution fusion | flops 536870912 | bytes 14680064 | tf_op jit(solution)/shard_map/while/body/gij,gjd->gid/dot_general | solution.py:43
  93.6 12.3 %scatter_fusion = f32[16,128,256]{2,1,0:T(8,128)S(1)} fusion(f32[16,128,256]{2,1,0:T(8,128)S(1)} %get-tuple-element.290, s32[64]{0:T(128)S(1)} %fusion.57, f32[64,128,256]{2,1,0:T(8,128)} %fusion.59), kind=kCustom, calls=%fused_computation.9.clone.1 | custom fusion | flops 2097152 | bytes 25166080 | tf_op jit(solution)/shard_map/while/body/scatter-add | solution.py:47
  107.5 4.4 gather_fusion.3
  111.9 5.5 %gather_fusion.1 = bf16[64,128,128]{2,1,0:T(8,128)(2,1)} fusion(bf16[256,128,128]{2,1,0:T(8,128)(2,1)} %get-tuple-element.308, s32[1024]{0:T(1024)S(1)} %pad_clamp_fusion.8), kind=kCustom, calls=%fused_computation.1.clone.1 | custom fusion | bytes 4194560 | tf_op jit(solution)/shard_map/while/body/gather | solution.py:36
  117.4 7.3 %fusion.59 = f32[64,128,256]{2,1,0:T(8,128)} fusion(bf16[64,128,128]{2,1,0:T(8,128)(2,1)} %gather_fusion.1, bf16[64,128,256]{2,1,0:T(8,128)(2,1)} %gather_fusion.3), kind=kOutput, calls=%fused_computation.95.clone.1 | convolution fusion | flops 536870912 | bytes 14680064 | tf_op jit(solution)/shard_map/while/body/gij,gjd->gid/dot_general | solution.py:43
  126.2 12.3 %scatter_fusion = f32[16,128,256]{2,1,0:T(8,128)S(1)} fusion(f32[16,128,256]{2,1,0:T(8,128)S(1)} %get-tuple-element.290, s32[64]{0:T(128)S(1)} %fusion.57, f32[64,128,256]{2,1,0:T(8,128)} %fusion.59), kind=kCustom, calls=%fused_computation.9.clone.1 | custom fusion | flops 2097152 | bytes 25166080 | tf_op jit(solution)/shard_map/while/body/scatter-add | solution.py:47
  140.0 4.4 gather_fusion.3
  144.4 5.5 %gather_fusion.1 = bf16[64,128,128]{2,1,0:T(8,128)(2,1)} fusion(bf16[256,128,128]{2,1,0:T(8,128)(2,1)} %get-tuple-element.308, s32[1024]{0:T(1024)S(1)} %pad_clamp_fusion.8), kind=kCustom, calls=%fused_computation.1.clone.1 | custom fusion | bytes 4194560 | tf_op jit(solution)/shard_map/while/body/gather | solution.py:36
  150.0 7.3 %fusion.59 = f32[64,128,256]{2,1,0:T(8,128)} fusion(bf16[64,128,128]{2,1,0:T(8,128)(2,1)} %gather_fusion.1, bf16[64,128,256]{2,1,0:T(8,128)(2,1)} %gather_fusion.3), kind=kOutput, calls=%fused_computation.95.clone.1 | convolution fusion | flops 536870912 | bytes 14680064 | tf_op jit(solution)/shard_map/while/body/gij,gjd->gid/dot_general | solution.py:43
  158.7 12.3 %scatter_fusion = f32[16,128,256]{2,1,0:T(8,128)S(1)} fusion(f32[16,128,256]{2,1,0:T(8,128)S(1)} %get-tuple-element.290, s32[64]{0:T(128)S(1)} %fusion.57, f32[64,128,256]{2,1,0:T(8,128)} %fusion.59), kind=kCustom, calls=%fused_computation.9.clone.1 | custom fusion | flops 2097152 | bytes 25166080 | tf_op jit(solution)/shard_map/while/body/scatter-add | solution.py:47
  172.5 6.9 %all_gather.21 = bf16[128,64]{1,0:T(8,128)(2,1)S(1)} all-gather(bf16[16,64]{1,0:T(8,128)(2,1)S(1)} %copy-done.14), channel_id=1, replica_groups=mesh['row'=8,'col'=4] {'row'}, dimensions={0}, use_global_device_ids=true | all-gather | bytes 18432 | tf_op jit(solution)/shard_map/all_gather | solution.py:83
  179.5 43.3 %scatter_custom_fusion.2 = f32[65536]{0:T(1024)S(1)} fusion(s32[8192]{0:T(1024)S(1)} %bitcast.89, f32[8192]{0:T(1024)S(1)} %reshape.262, f32[]{:T(128)} %constant.162.clone.1), kind=kCustom, calls=%fused_computation.48 | custom fusion | flops 8192 | bytes 262148 | tf_op jit(solution)/shard_map/scatter-add | solution.py:133
  222.8 10.4 %all_gather.22 = bf16[128,256]{1,0:T(8,128)(2,1)S(1)} all-gather(bf16[16,256]{1,0:T(8,128)(2,1)S(1)} %copy-done.10), channel_id=1, replica_groups=mesh['row'=8,'col'=4] {'row'}, dimensions={0}, use_global_device_ids=true | all-gather | bytes 73728 | tf_op jit(solution)/shard_map/all_gather | solution.py:81
  238.7 3.2 sort.32
  242.0 23.5 %all-gather.8.cloned.1.call-done = bf16[2048,256]{1,0:T(8,128)(2,1)} async-done(((bf16[512,256]{1,0:T(8,128)(2,1)}), bf16[2048,256]{1,0:T(8,128)(2,1)}) %all-gather.8.cloned.1.call-update) | async-done | bytes 1048592 | tf_op jit(solution)/shard_map/all_gather | solution.py:149
  265.5 2.5 broadcast_in_dim.69
  268.0 144.0 %while.21 = (s32[]{:T(128)}, f32[32,128,256]{2,1,0:T(8,128)}, s32[]{:T(128)}, s32[]{:T(128)}, s32[256]{0:T(256)S(1)}, /*index=5*/s32[256]{0:T(256)S(1)}, bf16[25...) while((s32[]{:T(128)}, f32[32,128,256]{2,1,0:T(8,128)}, ...), condition=%wide.region_15.16_spmd, body=%wide.region_13.15_spmd.sunk | while | flops 538970880 | bytes 52441528 | solution.py:50
  269.1 2.8 gather_fusion.7
  271.8 4.5 gather_fusion.5
  276.4 6.7 %fusion.64 = f32[64,128,256]{2,1,0:T(8,128)} fusion(bf16[64,128,128]{2,1,0:T(8,128)(2,1)S(1)} %gather_fusion.5, bf16[64,128,256]{2,1,0:T(8,128)(2,1)} %gather_fusion.7), kind=kOutput, calls=%fused_computation.96.clone.1 | convolution fusion | flops 536870912 | bytes 14680064 | tf_op jit(solution)/shard_map/while/body/gij,gid->gjd/dot_general | solution.py:39
  284.5 20.0 %scatter_fusion.1 = f32[32,128,256]{2,1,0:T(8,128)} fusion(f32[32,128,256]{2,1,0:T(8,128)} %get-tuple-element.329, s32[64]{0:T(128)S(1)} %fusion.62, f32[64,128,256]{2,1,0:T(8,128)} %fusion.64), kind=kCustom, calls=%fused_computation.10.clone.1 | custom fusion | flops 2097152 | bytes 25166080 | tf_op jit(solution)/shard_map/while/body/scatter-add | solution.py:47
  305.4 2.8 gather_fusion.7
  308.1 4.3 gather_fusion.5
  312.5 6.7 %fusion.64 = f32[64,128,256]{2,1,0:T(8,128)} fusion(bf16[64,128,128]{2,1,0:T(8,128)(2,1)S(1)} %gather_fusion.5, bf16[64,128,256]{2,1,0:T(8,128)(2,1)} %gather_fusion.7), kind=kOutput, calls=%fused_computation.96.clone.1 | convolution fusion | flops 536870912 | bytes 14680064 | tf_op jit(solution)/shard_map/while/body/gij,gid->gjd/dot_general | solution.py:39
  320.6 19.8 %scatter_fusion.1 = f32[32,128,256]{2,1,0:T(8,128)} fusion(f32[32,128,256]{2,1,0:T(8,128)} %get-tuple-element.329, s32[64]{0:T(128)S(1)} %fusion.62, f32[64,128,256]{2,1,0:T(8,128)} %fusion.64), kind=kCustom, calls=%fused_computation.10.clone.1 | custom fusion | flops 2097152 | bytes 25166080 | tf_op jit(solution)/shard_map/while/body/scatter-add | solution.py:47
  341.3 2.8 gather_fusion.7
  344.1 4.3 gather_fusion.5
  348.4 6.7 %fusion.64 = f32[64,128,256]{2,1,0:T(8,128)} fusion(bf16[64,128,128]{2,1,0:T(8,128)(2,1)S(1)} %gather_fusion.5, bf16[64,128,256]{2,1,0:T(8,128)(2,1)} %gather_fusion.7), kind=kOutput, calls=%fused_computation.96.clone.1 | convolution fusion | flops 536870912 | bytes 14680064 | tf_op jit(solution)/shard_map/while/body/gij,gid->gjd/dot_general | solution.py:39
  356.5 19.6 %scatter_fusion.1 = f32[32,128,256]{2,1,0:T(8,128)} fusion(f32[32,128,256]{2,1,0:T(8,128)} %get-tuple-element.329, s32[64]{0:T(128)S(1)} %fusion.62, f32[64,128,256]{2,1,0:T(8,128)} %fusion.64), kind=kCustom, calls=%fused_computation.10.clone.1 | custom fusion | flops 2097152 | bytes 25166080 | tf_op jit(solution)/shard_map/while/body/scatter-add | solution.py:47
  377.1 2.8 gather_fusion.7
  379.8 4.3 gather_fusion.5
  384.2 6.7 %fusion.64 = f32[64,128,256]{2,1,0:T(8,128)} fusion(bf16[64,128,128]{2,1,0:T(8,128)(2,1)S(1)} %gather_fusion.5, bf16[64,128,256]{2,1,0:T(8,128)(2,1)} %gather_fusion.7), kind=kOutput, calls=%fused_computation.96.clone.1 | convolution fusion | flops 536870912 | bytes 14680064 | tf_op jit(solution)/shard_map/while/body/gij,gid->gjd/dot_general | solution.py:39
  392.3 19.7 %scatter_fusion.1 = f32[32,128,256]{2,1,0:T(8,128)} fusion(f32[32,128,256]{2,1,0:T(8,128)} %get-tuple-element.329, s32[64]{0:T(128)S(1)} %fusion.62, f32[64,128,256]{2,1,0:T(8,128)} %fusion.64), kind=kCustom, calls=%fused_computation.10.clone.1 | custom fusion | flops 2097152 | bytes 25166080 | tf_op jit(solution)/shard_map/while/body/scatter-add | solution.py:47
  412.0 3.9 convert_element_type.39
  417.5 2.0 convolution_bitcast_fusion
  419.5 8.6 %gather_fusion.8 = f32[1024]{0:T(1024)S(1)} fusion(f32[16,4096]{1,0:T(8,128)S(1)} %convolution_bitcast_fusion, s32[1024]{0:T(1024)S(1)} %reshape.236), kind=kCustom, calls=%fused_computation.8 | custom fusion | bytes 16384 | tf_op jit(solution)/shard_map/jit(take_along_axis)/gather | solution.py:119
  428.7 26.2 %reduce-scatter.5.cloned.1.call-done = bf16[512,256]{1,0:T(8,128)(2,1)} async-done(((bf16[4096,256]{1,0:T(8,128)(2,1)}), bf16[512,256]{1,0:T(8,128)(2,1)}) %reduce-scatter.5.cloned.1.call-update) | async-done | bytes 262160 | tf_op jit(solution)/shard_map/reduce_scatter | solution.py:150
  454.9 2.0 convolution_add_fusion
  (134 shorter events, 32.1 us)
Async XLA Ops:
  7.2 226.3 %copy-start = (bf16[256,256]{1,0:T(8,128)(2,1)S(1)}, bf16[256,256]{1,0:T(8,128)(2,1)}, u32[]{:S(2)}) copy-start(bf16[256,256]{1,0:T(8,128)(2,1)} %param.21) | copy-start | bytes 393220
  7.2 33.4 %all-gather.4.cloned.1.call-start = ((), (), s32[]{:S(2)}) async-start(), calls=%async_computation.2 | async-start | bytes 2359296 | tf_op jit(solution)/shard_map/all_gather | solution.py:80
  7.9 225.6 %reduce-scatter.3.cloned.1.call-start = ((), (), s32[]{:S(2)}) async-start(), calls=%async_computation.3 | async-start | bytes 1310720 | tf_op jit(solution)/shard_map/reduce_scatter | solution.py:85
  52.3 7.3 %copy-start.2 = (s32[256]{0:T(256)S(1)}, s32[256]{0:T(256)}, u32[]{:S(2)}) copy-start(s32[256]{0:T(256)} %get-tuple-element.307) | copy-start | bytes 3076 | tf_op jit(solution)/shard_map/while
  84.9 7.3 %copy-start.2 = (s32[256]{0:T(256)S(1)}, s32[256]{0:T(256)}, u32[]{:S(2)}) copy-start(s32[256]{0:T(256)} %get-tuple-element.307) | copy-start | bytes 3076 | tf_op jit(solution)/shard_map/while
  117.4 7.3 %copy-start.2 = (s32[256]{0:T(256)S(1)}, s32[256]{0:T(256)}, u32[]{:S(2)}) copy-start(s32[256]{0:T(256)} %get-tuple-element.307) | copy-start | bytes 3076 | tf_op jit(solution)/shard_map/while
  150.0 7.3 %copy-start.2 = (s32[256]{0:T(256)S(1)}, s32[256]{0:T(256)}, u32[]{:S(2)}) copy-start(s32[256]{0:T(256)} %get-tuple-element.307) | copy-start | bytes 3076 | tf_op jit(solution)/shard_map/while
  171.0 1.5 copy-start.14
  171.0 51.8 %copy-start.10 = (bf16[16,256]{1,0:T(8,128)(2,1)S(1)}, bf16[16,256]{1,0:T(8,128)(2,1)}, u32[]{:S(2)}) copy-start(bf16[16,256]{1,0:T(8,128)(2,1)} %param.28) | copy-start | bytes 24580
  171.0 62.2 %copy-start.6 = (bf16[512,256]{1,0:T(8,128)(2,1)S(1)}, bf16[512,256]{1,0:T(8,128)(2,1)}, u32[]{:S(2)}) copy-start(bf16[512,256]{1,0:T(8,128)(2,1)} %param.19) | copy-start | bytes 786436
  171.0 62.2 %copy-start.7 = (bf16[256,256]{1,0:T(8,128)(2,1)S(1)}, bf16[256,256]{1,0:T(8,128)(2,1)}, u32[]{:S(2)}) copy-start(bf16[256,256]{1,0:T(8,128)(2,1)} %param.20) | copy-start | bytes 393220
  171.0 62.5 %copy-start.15 = (f32[256]{0:T(256)S(1)}, f32[256]{0:T(256)}, u32[]{:S(2)}) copy-start(f32[256]{0:T(256)} %param.22) | copy-start | bytes 3076
  171.1 63.7 %copy-start.16 = (f32[256]{0:T(256)S(1)}, f32[256]{0:T(256)}, u32[]{:S(2)}) copy-start(f32[256]{0:T(256)} %param.23) | copy-start | bytes 3076
  172.2 93.3 %all-gather.8.cloned.1.call-start = ((), (), s32[]{:S(2)}) async-start(), calls=%async_computation.5 | async-start | bytes 1310720 | tf_op jit(solution)/shard_map/all_gather | solution.py:149
  235.3 32.7 %copy-start.1 = (s32[256]{0:T(256)S(1)}, s32[256]{0:T(256)}, u32[]{:S(2)}) copy-start(s32[256]{0:T(256)} %get-tuple-element.359) | copy-start | bytes 3076
  235.3 32.7 %copy-start.3 = (s32[256]{0:T(256)S(1)}, s32[256]{0:T(256)}, u32[]{:S(2)}) copy-start(s32[256]{0:T(256)} %get-tuple-element.360) | copy-start | bytes 3076
  237.4 180.1 %all-gather.6.cloned.1.call-start = ((), (), s32[]{:S(2)}) async-start(), calls=%async_computation.4 | async-start | bytes 2359296 | tf_op jit(solution)/shard_map/all_gather | solution.py:114
  241.9 213.0 %reduce-scatter.5.cloned.1.call-start = ((), (), s32[]{:S(2)}) async-start(), calls=%async_computation.6 | async-start | bytes 2359296 | tf_op jit(solution)/shard_map/reduce_scatter | solution.py:150
  265.5 2.5 copy-start.4
  412.0 4.0 copy-start.9
  412.0 4.1 copy-start.12
  412.0 4.1 copy-start.17
  412.0 4.2 copy-start.13
  412.0 4.6 copy-start.5
  412.0 5.4 %copy-start.11 = (bf16[16,256]{1,0:T(8,128)(2,1)S(1)}, bf16[16,256]{1,0:T(8,128)(2,1)}, u32[]{:S(2)}) copy-start(bf16[16,256]{1,0:T(8,128)(2,1)} %param.28) | copy-start | bytes 24580
  419.5 35.5 %copy-start.8 = (bf16[256,256]{1,0:T(8,128)(2,1)S(1)}, bf16[256,256]{1,0:T(8,128)(2,1)}, u32[]{:S(2)}) copy-start(bf16[256,256]{1,0:T(8,128)(2,1)} %param.20) | copy-start | bytes 393220
Sparse Core Ops, SparseCore 0:
  9.9 30.6 all-gather.3
  172.3 26.2 reduce-scatter.2
  237.5 27.9 all-gather.7
  268.0 27.6 all-gather.5
  416.1 38.7 reduce-scatter.4
where the time goes:
time: 466 us; the launch traced here: 463 us
  other arithmetic  193 us (41%)
  local copies, waits for them, and re-layouts  96.1 us (21%)
  waiting for transfers between devices  66.5 us (14%)
  matrix products  63.1 us (14%)
  blocking collectives  28.1 us (6%)
  between operations  16 us (3%)
    scatter-add x8, other arithmetic, add_group(): return summed.at[segment].add(product, mode='drop')  128 us
    scatter-add x1, other arithmetic, body(): weights.at[flat_index.reshape(-1)]  43.3 us
    gather x8, local copies, waits for them, and re-layouts, add_group(): tile_group = tile_set[picked]  39.6 us
    gather x16, local copies, waits for them, and re-layouts, add_group(): source_rows = shaped[sources[picked]]  37.7 us
    dot_general x4, matrix products, add_group(): jnp.einsum('gij,gjd->gid', tile_group, source_rows, preferred_element_typ...  29.2 us
    dot_general x4, matrix products, add_group(): jnp.einsum('gij,gid->gjd', tile_group, source_rows, preferred_element_typ...  26.9 us
    reduce_scatter x1, waiting for transfers between devices, body(): lax.psum_scatter(block_products(tile_set, tile_cols, tile_rows, live_coun...  26.2 us
    all_gather x1, waiting for transfers between devices, body(): range_source = lax.all_gather(back_source, 'col', axis=0, tiled=True)  23.5 us
  transfers between devices with their start and end apart: 5, of which 3 were waited for; matrix products, arithmetic and copies ran while one was open for 46% of the time, Pallas kernels for 0%

commit v1 on v0

v1 whole, which is shorter than its diff:
```python
import functools

import jax
import jax.numpy as jnp
from jax import lax
from jax.experimental import pallas as pl
from jax.experimental.pallas import tpu as pltpu
from jax.sharding import PartitionSpec as P

norm_eps = 1e-05
f32 = jnp.float32
bf16 = jnp.bfloat16
VMEM_LIMIT = 56 * 1024 * 1024


def dot(a, b, dims=((1,), (0,))):
    return lax.dot_general(a, b, (dims, ((), ())), preferred_element_type=f32)


def block_kernel(
    transpose, chunk, unroll, targets, sources, count, tiles, source, out, total
):
    step = pl.program_id(0)
    target_blocks = out.shape[0]

    @pl.when(step == 0)
    def _():
        total[...] = jnp.zeros_like(total)

    live = jnp.clip(count[0] - step * chunk, 0, chunk)

    def group(index, carry):
        for lane in range(unroll):
            slot = index * unroll + lane
            place = step * chunk + slot
            target = jnp.where(slot < live, targets[place], target_blocks)
            dims = ((0,), (0,)) if transpose else ((1,), (0,))
            total[target] += dot(tiles[slot], source[sources[place]], dims)
        return carry

    lax.fori_loop(0, (live + unroll - 1) // unroll, group, 0)

    @pl.when(step == pl.num_programs(0) - 1)
    def _():
        out[...] = total[0:target_blocks].astype(out.dtype)


def block_products(tiles, targets, sources, count, source, target_blocks, transpose):
    slots, block, _ = tiles.shape
    width = source.shape[-1]
    chunk = min(32, slots)
    shaped = source.reshape(-1, block, width)
    return pl.pallas_call(
        functools.partial(block_kernel, transpose, chunk, 4),
        grid_spec=pltpu.PrefetchScalarGridSpec(
            num_scalar_prefetch=3,
            grid=(slots // chunk,),
            in_specs=[
                pl.BlockSpec((chunk, block, block), lambda i, *_: (i, 0, 0)),
                pl.BlockSpec(shaped.shape, lambda i, *_: (0, 0, 0)),
            ],
            out_specs=pl.BlockSpec((target_blocks, block, width), lambda i, *_: (0, 0, 0)),
            scratch_shapes=[pltpu.VMEM((target_blocks + 1, block, width), f32)],
        ),
        out_shape=jax.ShapeDtypeStruct((target_blocks, block, width), bf16),
        compiler_params=pltpu.CompilerParams(vmem_limit_bytes=VMEM_LIMIT),
        name="block_products",
    )(targets, sources, count, tiles, shaped).reshape(target_blocks * block, width)


def weights_of(ids, cot, weights):
    rows = min(128, weights.shape[0])
    queries = weights.shape[1]

    def part(index, carry):
        start = index * rows
        numbers = lax.broadcasted_iota(jnp.int32, (rows, queries), 0) + start
        acc = jnp.zeros((rows, queries), f32)
        for k in range(ids.shape[0]):
            acc += jnp.where(numbers == ids[k : k + 1, :], cot[k : k + 1, :], 0.0)
        weights[pl.ds(pl.multiple_of(start, rows), rows), :] = acc
        return carry

    lax.fori_loop(0, weights.shape[0] // rows, part, 0)


def picked_scores(ids, table, picks, raw):
    rows = min(128, table.shape[0])
    queries = table.shape[1]
    picks[...] = jnp.zeros_like(picks)

    def part(index, carry):
        start = index * rows
        numbers = lax.broadcasted_iota(jnp.int32, (rows, queries), 0) + start
        values = table[pl.ds(pl.multiple_of(start, rows), rows), :]
        for k in range(ids.shape[0]):
            hit = jnp.where(numbers == ids[k : k + 1, :], values, 0.0)
            picks[k] += jnp.sum(hit.reshape(rows // 8, 8, queries), axis=0)
        return carry

    lax.fori_loop(0, table.shape[0] // rows, part, 0)
    raw[...] = jnp.sum(picks[...], axis=1)


def node_math(items, aggregate, w_self, w_neighbor, bias, gain, weights, queries):
    width = items.shape[1]
    preact = dot(items, w_self) + dot(aggregate.astype(bf16), w_neighbor) + bias
    gate = 1.0 / (1.0 + jnp.exp(-preact))
    active = preact * gate
    scale = lax.rsqrt(jnp.mean(active * active, axis=-1, keepdims=True) + norm_eps)
    hidden = (gain * active * scale).astype(bf16)
    high = weights.astype(bf16)
    low = (weights - high.astype(f32)).astype(bf16)
    grad_hidden = (dot(high, queries) + dot(low, queries)) * (width ** -0.5)
    scaled = gain * grad_hidden
    along = jnp.sum(scaled * active, axis=-1, keepdims=True) * (1.0 / width)
    grad_active = scale * scaled - active * (scale * scale * scale * along)
    grad_preact = grad_active * (gate * (1.0 + preact * (1.0 - gate)))
    return hidden, grad_preact.astype(bf16)


def node_kernel(
    items, aggregate, w_self, w_neighbor, bias, gain, queries, ids, cot,
    hidden, grad_self, back_source, raw, weights, table, picks,
):
    weights_of(ids, cot, weights)
    new, grad = node_math(
        items[...], aggregate[...], w_self[...], w_neighbor[...], bias[...], gain[...],
        weights[...], queries[...],
    )
    hidden[...] = new
    last = ((1,), (1,))
    back_source[...] = dot(grad, w_neighbor[...], last).astype(bf16)
    grad_self[...] = dot(grad, w_self[...], last)
    table[...] = dot(new, queries[...], last)
    picked_scores(ids, table, picks, raw)


def node_step(items, aggregate, w_self, w_neighbor, bias, gain, queries, ids, cot):
    rows, width = items.shape
    requests = queries.shape[0]
    cands = ids.shape[0]
    return pl.pallas_call(
        node_kernel,
        out_shape=(
            jax.ShapeDtypeStruct((rows, width), bf16),
            jax.ShapeDtypeStruct((rows, width), f32),
            jax.ShapeDtypeStruct((rows, width), bf16),
            jax.ShapeDtypeStruct((cands, requests), f32),
        ),
        scratch_shapes=[
            pltpu.VMEM((rows, requests), f32),
            pltpu.VMEM((rows, requests), f32),
            pltpu.VMEM((cands, 8, requests), f32),
        ],
        compiler_params=pltpu.CompilerParams(vmem_limit_bytes=VMEM_LIMIT),
        name="node_step",
    )(items, aggregate, w_self, w_neighbor, bias[None], gain[None], queries, ids, cot)


def body(
    item_features,
    self_weight,
    neighbor_weight,
    layer_bias,
    norm_gain,
    blocks,
    block_rows,
    block_cols,
    counts,
    queries,
    candidates,
    positions,
    position_table,
    tower_weight,
    score_cotangent,
):
    rows_dev, width = item_features.shape
    tiles = blocks[0, 0]
    block = tiles.shape[1]
    cands = candidates.shape[1]
    col_count = lax.axis_size("col")
    row_count = lax.axis_size("row")
    column_items = lax.all_gather(item_features, "row", axis=0, tiled=True)
    packed = jnp.concatenate(
        [queries.astype(f32), candidates.astype(f32), score_cotangent.astype(f32)], axis=1
    )
    packed = lax.all_gather(packed, "row", axis=0, tiled=True)
    all_queries = packed[:, :width].astype(bf16)
    all_ids = packed[:, width : width + cands].astype(jnp.int32).T
    all_cot = packed[:, width + cands :].T
    my_piece = lax.axis_index("row") * col_count + lax.axis_index("col")
    local_ids = jnp.where(all_ids // rows_dev == my_piece, all_ids % rows_dev, -1)

    parts = block_products(
        tiles, block_rows[0, 0], block_cols[0, 0], counts[0],
        column_items, col_count * rows_dev // block, False,
    )
    aggregate = lax.psum_scatter(parts, "col", scatter_dimension=0, tiled=True)
    hidden, grad_self, back_source, raw = node_step(
        item_features, aggregate, self_weight, neighbor_weight, layer_bias, norm_gain,
        all_queries, local_ids, all_cot,
    )
    range_source = lax.all_gather(back_source, "col", axis=0, tiled=True)
    back_parts = block_products(
        tiles, block_cols[0, 0], block_rows[0, 0], counts[0],
        range_source, row_count * rows_dev // block, True,
    )
    raw_scores = lax.psum_scatter(raw.T, "row", scatter_dimension=0, tiled=True)
    tower_values = jnp.sum(jax.nn.relu(position_table) * tower_weight, axis=-1)
    position_hits = positions[..., None] == jnp.arange(tower_values.shape[0])
    scores = raw_scores * width ** (-0.5) + jnp.sum(
        jnp.where(position_hits, tower_values, 0.0), axis=-1
    )
    back_sum = lax.psum_scatter(back_parts, "row", scatter_dimension=0, tiled=True)
    return (hidden, scores, grad_self + back_sum.astype(f32))


def solution(mesh):
    in_specs = (
        P(("row", "col"), None),
        P(),
        P(),
        P(),
        P(),
        P("row", "col", None, None, None),
        P("row", "col", None),
        P("row", "col", None),
        P("row", "col"),
        P(("row", "col"), None),
        P(("row", "col"), None),
        P(("row", "col"), None),
        P(),
        P(),
        P(("row", "col"), None),
    )
    out_specs = (P(("row", "col"), None), P(("row", "col"), None), P(("row", "col"), None))
    return jax.shard_map(body, mesh=mesh, in_specs=in_specs, out_specs=out_specs, check_vma=False)
```

time: 466 us -> 209 us (0.45)
  other arithmetic: 193 us -> 4.33 us
  local copies, waits for them, and re-layouts: 96.1 us -> 3.68 us
  waiting for transfers between devices: 66.5 us -> 140 us
  matrix products: 63.1 us -> 0 us
  Pallas kernels: 0 us -> 32.2 us
  blocking collectives: 28.1 us -> 13.7 us
    scatter-add x9 -> x0, other arithmetic: 171 us -> none  [the longest x8 128 us: add_group(): return summed.at[segment].add(product, mode='drop')]
    gather x35 -> x0, local copies, waits for them, and re-layouts: 92.3 us -> none  [the longest x8 39.6 us: add_group(): tile_group = tile_set[picked]]
    dot_general x14 -> x0, matrix products: 63.1 us -> none  [the longest x4 29.2 us: add_group(): jnp.einsum('gij,gjd->gid', tile_group, source_rows, preferred_element_typ...]
    reduce_scatter x2 -> x3, waiting for transfers between devices: 26.2 us -> 81.8 us  [the longest x1 43.1 us: body(): lax.psum_scatter(back_parts, 'row', scatter_dimension=0, tiled=True)]
    pallas_call x0 -> x3, Pallas kernels: none -> 32.2 us  [the longest x2 26 us: block_products(): pl.pallas_call(functools.partial(block_kernel, transpose, chunk, 4), grid...]
    all_gather x2 -> x1, waiting for transfers between devices: 16 us -> 31.9 us  [body(): column_items = lax.all_gather(item_features, 'row', axis=0, tiled=True)]
    all_gather x3 -> x1, blocking collectives: 28.1 us -> 13.7 us  [body(): packed = lax.all_gather(packed, 'row', axis=0, tiled=True)]
    sort x2 -> x0, other arithmetic: 6.33 us -> none  [block_products(): jnp.argsort(jnp.where(is_live, slot_index, slot_total + slot_index))]
  transfers between devices with their start and end apart: 5 -> 5, of which waited for: 3 -> 5; matrix products, arithmetic and copies ran while one was open for 46% -> 3% of each run, Pallas kernels for 0% -> 6%
where the time goes in v1:
time: 209 us; the launch traced here: 208 us
  waiting for transfers between devices  140 us (67%)
  Pallas kernels  32.2 us (15%)
  between operations  14.5 us (7%)
  blocking collectives  13.7 us (7%)
  other arithmetic  4.33 us (2%)
  local copies, waits for them, and re-layouts  3.68 us (2%)
    reduce_scatter x1, waiting for transfers between devices, body(): lax.psum_scatter(back_parts, 'row', scatter_dimension=0, tiled=True)  43.1 us
    all_gather x1, waiting for transfers between devices, body(): column_items = lax.all_gather(item_features, 'row', axis=0, tiled=True)  31.9 us
    pallas_call x2, Pallas kernels, block_products(): pl.pallas_call(functools.partial(block_kernel, transpose, chunk, 4), grid...  26 us
    all_gather x1, waiting for transfers between devices, body(): range_source = lax.all_gather(back_source, 'col', axis=0, tiled=True)  25.1 us
    reduce_scatter x1, waiting for transfers between devices, body(): raw_scores = lax.psum_scatter(raw.T, 'row', scatter_dimension=0, tiled=True)  21.1 us
    reduce_scatter x1, waiting for transfers between devices, body(): aggregate = lax.psum_scatter(parts, 'col', scatter_dimension=0, tiled=True)  17.6 us
    all_gather x1, blocking collectives, body(): packed = lax.all_gather(packed, 'row', axis=0, tiled=True)  13.7 us
    pallas_call x1, Pallas kernels, node_step(): pl.pallas_call(node_kernel, out_shape=(jax.ShapeDtypeStruct((rows, width)...  6.23 us
  transfers between devices with their start and end apart: 5, of which 5 were waited for; matrix products, arithmetic and copies ran while one was open for 3% of the time, Pallas kernels for 6%

profile of v1, /device:TPU:0, one launch (start us, length us, event | category | flops | bytes accessed | tf_op | source)
XLA Modules:
  0.0 208.2 jit_solution(3281171744365273328)
XLA Ops:
  7.2 0.0 all-gather.3.cloned.1.call-start
  7.2 0.7 all-gather.3.cloned.1.call-update
  7.9 0.0 reduce-scatter.6.cloned.1.call-start
  8.6 31.9 %all-gather.3.cloned.1.call-done = bf16[4096,256]{1,0:T(8,128)(2,1)} async-done(((bf16[512,256]{1,0:T(8,128)(2,1)}), bf16[4096,256]{1,0:T(8,128)(2,1)}) %all-gather.3.cloned.1.call-update) | async-done | bytes 2097168 | tf_op jit(solution)/shard_map/all_gather | solution.py:184
  40.5 0.0 copy-start.3
  40.5 0.0 copy-start.5
  40.5 0.0 copy-start.2
  40.5 12.5 %block_products.2 = bf16[16,128,256]{2,1,0:T(8,128)(2,1)} custom-call(s32[256]{0:T(256)} %bitcast.49, s32[256]{0:T(256)} %bitcast.51, s32[1]{0:T(128)} %bitcast.39.count, bf16[256,128,128]{2,1,0:T(8,128)(2,1)} %bitcast.41, bf16[32,128,256]{2,1,0:T(8,128)(2,1)} %bitcast.45), custom_call_target="tpu_custom_call" | custom-call | tf_op jit(solution)/shard_map/block_products/pallas_call | solution.py:53
  53.0 0.0 reduce-scatter.6.cloned.1.call-update
  53.0 0.0 all-gather.5.cloned.1.call-start
  53.1 0.0 copy-done.3
  53.1 0.0 copy-done.5
  53.1 0.0 copy-done.2
  53.1 0.1 pad_maximum_fusion
  53.2 13.7 %all_gather.10 = f32[128,384]{1,0:T(8,128)S(1)} all-gather(f32[16,384]{1,0:T(8,128)S(1)} %pad_maximum_fusion), channel_id=1, replica_groups=mesh['row'=8,'col'=4] {'row'}, dimensions={0}, use_global_device_ids=true | all-gather | bytes 221184 | tf_op jit(solution)/shard_map/all_gather | solution.py:188
  66.9 0.6 slice.17.queries
  67.5 0.1 fusion.5
  67.6 0.7 copy.32
  68.3 0.1 copy.31
  68.3 0.7 fusion.1.ids
  69.0 17.6 %reduce-scatter.6.cloned.1.call-done.aggregate = bf16[512,256]{1,0:T(8,128)(2,1)} async-done(((bf16[2048,256]{1,0:T(8,128)(2,1)}), bf16[512,256]{1,0:T(8,128)(2,1)}) %reduce-scatter.6.cloned.1.call-update) | async-done | bytes 262160 | tf_op jit(solution)/shard_map/reduce_scatter | solution.py:199
  86.6 6.2 %node_step.1 = (bf16[512,256]{1,0:T(8,128)(2,1)}, f32[512,256]{1,0:T(8,128)}, bf16[512,256]{1,0:T(8,128)(2,1)}, f32[64,128]{1,0:T(8,128)}) custom-call(bf16[512,256]{1,0:T(8,128)(2,1)} %items.1, bf16[512,256]{1,0:T(8,128)(2,1)} %reduce-scatter.6.cloned.1.call-done.aggregate, bf16[256,256]{1,0:T(8,128)(2,1)} %w_self.1, bf16[256,256]{1,0:T(8,128)(2,1)} %w_neighbor.1, ...), custom_call_target="tpu_custom_call" | custom-call | tf_op jit(solution)/shard_map/node_step/pallas_call | solution.py:143
  92.8 0.0 all-gather.5.cloned.1.call-update
  92.9 0.0 reduce-scatter.10.cloned.1.call-start
  92.9 1.5 copy.29
  94.4 0.0 reduce-scatter.10.cloned.1.call-update
  94.4 0.0 reduce-scatter.8.cloned.1.call-start
  94.5 25.1 %all-gather.5.cloned.1.call-done = bf16[2048,256]{1,0:T(8,128)(2,1)} async-done(((bf16[512,256]{1,0:T(8,128)(2,1)}), bf16[2048,256]{1,0:T(8,128)(2,1)}) %all-gather.5.cloned.1.call-update) | async-done | bytes 1048592 | tf_op jit(solution)/shard_map/all_gather | solution.py:204
  119.6 13.5 %block_products.3 = bf16[32,128,256]{2,1,0:T(8,128)(2,1)} custom-call(s32[256]{0:T(256)} %bitcast.52, s32[256]{0:T(256)} %bitcast.50, s32[1]{0:T(128)} %bitcast.40.count, bf16[256,128,128]{2,1,0:T(8,128)(2,1)} %bitcast.42, bf16[16,128,256]{2,1,0:T(8,128)(2,1)} %bitcast.46), custom_call_target="tpu_custom_call" | custom-call | tf_op jit(solution)/shard_map/block_products/pallas_call | solution.py:53
  133.1 0.0 copy-start.1
  133.1 0.0 copy-start.6
  133.1 0.0 copy-start.4
  133.1 0.0 copy-start
  133.1 0.0 reduce-scatter.8.cloned.1.call-update
  133.1 0.7 copy-done.1
  133.8 0.0 copy-done.6
  133.8 0.1 multiply_reduce_fusion
  134.0 0.0 copy-done.4
  134.0 0.4 select_reduce_fusion
  134.4 21.1 %reduce-scatter.10.cloned.1.call-done = f32[16,64]{1,0:T(8,128)} async-done(((f32[128,64]{1,0:T(8,128)}), f32[16,64]{1,0:T(8,128)}) %reduce-scatter.10.cloned.1.call-update) | async-done | bytes 4112 | tf_op jit(solution)/shard_map/reduce_scatter | solution.py:209
  155.5 1.3 multiply_add_fusion
  156.8 43.1 %reduce-scatter.8.cloned.1.call-done = bf16[512,256]{1,0:T(8,128)(2,1)} async-done(((bf16[4096,256]{1,0:T(8,128)(2,1)}), bf16[512,256]{1,0:T(8,128)(2,1)}) %reduce-scatter.8.cloned.1.call-update) | async-done | bytes 262160 | tf_op jit(solution)/shard_map/reduce_scatter | solution.py:215
  199.9 0.0 copy-done
  199.9 1.8 convert_add_fusion
  (3 shorter events, 0.0 us)
Async XLA Ops:
  7.2 33.4 %all-gather.3.cloned.1.call-start = ((), (), s32[]{:S(2)}) async-start(), calls=%async_computation.3 | async-start | bytes 2359296 | tf_op jit(solution)/shard_map/all_gather | solution.py:184
  7.9 78.7 %reduce-scatter.6.cloned.1.call-start = ((), (), s32[]{:S(2)}) async-start(), calls=%async_computation.4 | async-start | bytes 1310720 | tf_op jit(solution)/shard_map/reduce_scatter | solution.py:199
  40.5 12.6 %copy-start.3 = (s32[16,64]{1,0:T(8,128)S(1)}, s32[16,64]{1,0:T(8,128)}, u32[]{:S(2)}) copy-start(s32[16,64]{1,0:T(8,128)} %param.25) | copy-start | bytes 12292
  40.5 12.6 %copy-start.5 = (bf16[16,64]{1,0:T(8,128)(2,1)S(1)}, bf16[16,64]{1,0:T(8,128)(2,1)}, u32[]{:S(2)}) copy-start(bf16[16,64]{1,0:T(8,128)(2,1)} %param.29) | copy-start | bytes 6148
  40.5 12.6 %copy-start.2 = (bf16[16,256]{1,0:T(8,128)(2,1)S(1)}, bf16[16,256]{1,0:T(8,128)(2,1)}, u32[]{:S(2)}) copy-start(bf16[16,256]{1,0:T(8,128)(2,1)} %param.24) | copy-start | bytes 24580
  53.0 66.6 %all-gather.5.cloned.1.call-start = ((), (), s32[]{:S(2)}) async-start(), calls=%async_computation.5 | async-start | bytes 1310720 | tf_op jit(solution)/shard_map/all_gather | solution.py:204
  92.9 62.6 %reduce-scatter.10.cloned.1.call-start = ((), (), s32[]{:S(2)}) async-start(), calls=%async_computation.7 | async-start | bytes 73728 | tf_op jit(solution)/shard_map/reduce_scatter | solution.py:209
  94.4 105.4 %reduce-scatter.8.cloned.1.call-start = ((), (), s32[]{:S(2)}) async-start(), calls=%async_computation.6 | async-start | bytes 2359296 | tf_op jit(solution)/shard_map/reduce_scatter | solution.py:215
  133.1 0.8 copy-start.1
  133.1 0.8 copy-start.6
  133.1 0.9 copy-start.4
  133.1 66.8 %copy-start = (f32[512,256]{1,0:T(8,128)S(1)}, f32[512,256]{1,0:T(8,128)}, u32[]{:S(2)}) copy-start(f32[512,256]{1,0:T(8,128)} %get-tuple-element.9) | copy-start | bytes 1572868
Sparse Core Ops, SparseCore 0:
  9.9 30.5 all-gather.2
  53.1 33.4 reduce-scatter.5
  93.0 26.5 all-gather.4
  122.7 32.7 reduce-scatter.9
  158.6 41.1 reduce-scatter.7

commit v2 on v1

--- a/solution.py
+++ b/solution.py
@@ -68,40 +68,6 @@
     )(targets, sources, count, tiles, shaped).reshape(target_blocks * block, width)
 
 
-def weights_of(ids, cot, weights):
-    rows = min(128, weights.shape[0])
-    queries = weights.shape[1]
-
-    def part(index, carry):
-        start = index * rows
-        numbers = lax.broadcasted_iota(jnp.int32, (rows, queries), 0) + start
-        acc = jnp.zeros((rows, queries), f32)
-        for k in range(ids.shape[0]):
-            acc += jnp.where(numbers == ids[k : k + 1, :], cot[k : k + 1, :], 0.0)
-        weights[pl.ds(pl.multiple_of(start, rows), rows), :] = acc
-        return carry
-
-    lax.fori_loop(0, weights.shape[0] // rows, part, 0)
-
-
-def picked_scores(ids, table, picks, raw):
-    rows = min(128, table.shape[0])
-    queries = table.shape[1]
-    picks[...] = jnp.zeros_like(picks)
-
-    def part(index, carry):
-        start = index * rows
-        numbers = lax.broadcasted_iota(jnp.int32, (rows, queries), 0) + start
-        values = table[pl.ds(pl.multiple_of(start, rows), rows), :]
-        for k in range(ids.shape[0]):
-            hit = jnp.where(numbers == ids[k : k + 1, :], values, 0.0)
-            picks[k] += jnp.sum(hit.reshape(rows // 8, 8, queries), axis=0)
-        return carry
-
-    lax.fori_loop(0, table.shape[0] // rows, part, 0)
-    raw[...] = jnp.sum(picks[...], axis=1)
-
-
 def node_math(items, aggregate, w_self, w_neighbor, bias, gain, weights, queries):
     width = items.shape[1]
     preact = dot(items, w_self) + dot(aggregate.astype(bf16), w_neighbor) + bias
@@ -119,41 +85,308 @@
     return hidden, grad_preact.astype(bf16)
 
 
+def remote(src, dst, send, recv, place):
+    return pltpu.make_async_remote_copy(
+        src_ref=src, dst_ref=dst, send_sem=send, recv_sem=recv,
+        device_id=place, device_id_type=pl.DeviceIdType.MESH,
+    )
+
+
+def greet(places):
+    barrier = pltpu.get_barrier_semaphore()
+    for place in places:
+        pl.semaphore_signal(
+            barrier, inc=1, device_id=place, device_id_type=pl.DeviceIdType.MESH
+        )
+    pl.semaphore_wait(barrier, len(places))
+
+
+def row_places(chips):
+    me = lax.axis_index("row")
+    core = lax.rem(me, 2)
+    chip = me // 2
+    ahead = [lax.rem(chip + i, chips) for i in range(chips)]
+    behind = [lax.rem(chip + chips - i, chips) for i in range(chips)]
+    return me, core, ahead, behind
+
+
+def gather_kernel(chips, *refs):
+    arrays = len(refs) // 2 - 1
+    inputs, outputs = refs[:arrays], refs[arrays : 2 * arrays]
+    send, recv = refs[2 * arrays :]
+    me, core, ahead, behind = row_places(chips)
+    sibling = {"row": me + 1 - 2 * core}
+    peers = [{"row": ahead[i] * 2 + core} for i in range(chips)]
+    greet(peers[1:] + [sibling])
+    copies = []
+    for n in range(arrays):
+        for i in range(1, chips):
+            copy = remote(
+                inputs[n], outputs[n].at[me], send.at[n, i], recv.at[n, i], peers[i]
+            )
+            copy.start()
+            copies.append(copy)
+    for n in range(arrays):
+        copy = remote(
+            inputs[n], outputs[n].at[me], send.at[n, chips], recv.at[n, chips], sibling
+        )
+        copy.start()
+        copies.append(copy)
+    own = [
+        pltpu.make_async_copy(inputs[n], outputs[n].at[me], send.at[n, 0])
+        for n in range(arrays)
+    ]
+    for copy in own:
+        copy.start()
+    forwards = []
+    for n in reversed(range(arrays)):
+        for i in range(1, chips):
+            copies[n * (chips - 1) + i - 1].wait_recv()
+            piece = outputs[n].at[behind[i] * 2 + core]
+            copy = remote(
+                piece, piece, send.at[n, chips + i], recv.at[n, chips + i], sibling
+            )
+            copy.start()
+            forwards.append(copy)
+    for copy in copies[arrays * (chips - 1) :]:
+        copy.wait_recv()
+    for copy in forwards:
+        copy.wait_recv()
+    for copy in copies + forwards:
+        copy.wait_send()
+    for copy in own:
+        copy.wait()
+
+
+def gather_rows(row_count, *arrays):
+    chips = row_count // 2
+    return pl.pallas_call(
+        functools.partial(gather_kernel, chips),
+        out_shape=tuple(
+            jax.ShapeDtypeStruct((row_count,) + array.shape, array.dtype) for array in arrays
+        ),
+        in_specs=[pl.BlockSpec(memory_space=pl.ANY)] * len(arrays),
+        out_specs=tuple(pl.BlockSpec(memory_space=pl.ANY) for _ in arrays),
+        scratch_shapes=[
+            pltpu.SemaphoreType.DMA((len(arrays), 2 * chips)),
+            pltpu.SemaphoreType.DMA((len(arrays), 2 * chips)),
+        ],
+        compiler_params=pltpu.CompilerParams(
+            collective_id=0, has_side_effects=True, vmem_limit_bytes=VMEM_LIMIT
+        ),
+        name="gather_rows",
+    )(*arrays)
+
+
+def scatter_kernel(
+    chips, scale, parts, raw, grad_self, position_scores, grads, scores,
+    near, sums, far, near_raw, sums_raw, far_raw, send, recv,
+):
+    me, core, ahead, behind = row_places(chips)
+    sibling = {"row": me + 1 - 2 * core}
+    peers = [{"row": ahead[i] * 2 + core} for i in range(chips)]
+    greet(peers[1:] + [sibling])
+    order = list(range(1, chips)) + [0]
+    arrays = ((parts, near, sums, far), (raw, near_raw, sums_raw, far_raw))
+    first = {}
+    for i in order:
+        for n, (mine, inbox, _, _) in enumerate(arrays):
+            copy = remote(
+                mine.at[ahead[i] * 2 + 1 - core], inbox.at[i],
+                send.at[n, i], recv.at[n, i], sibling,
+            )
+            copy.start()
+            first[n, i] = copy
+    second = []
+    for i in order:
+        for n, (mine, inbox, summed, outbox) in enumerate(arrays):
+            first[n, i].wait_recv()
+            value = mine[ahead[i] * 2 + core].astype(f32) + inbox[i].astype(f32)
+            if i == 0:
+                if n == 0:
+                    grads[...] = grad_self[...] + value
+                else:
+                    scores[...] = value
+            else:
+                summed[i] = value.astype(summed.dtype)
+                copy = remote(
+                    summed.at[i], outbox.at[i],
+                    send.at[n, chips + i], recv.at[n, chips + i], peers[i],
+                )
+                copy.start()
+                second.append((n, i, copy))
+    for n, i, copy in second:
+        copy.wait_recv()
+        if n == 0:
+            grads[...] += far[i].astype(f32)
+        else:
+            scores[...] += far_raw[i]
+    scores[...] = scores[...] * scale + position_scores[...]
+    for copy in first.values():
+        copy.wait_send()
+    for _, _, copy in second:
+        copy.wait_send()
+
+
+def scatter_rows(row_count, parts, raw, grad_self, position_scores, scale):
+    chips = row_count // 2
+    part = parts.shape[1:]
+    part_raw = raw.shape[1:]
+    return pl.pallas_call(
+        functools.partial(scatter_kernel, chips, scale),
+        out_shape=(
+            jax.ShapeDtypeStruct(grad_self.shape, f32),
+            jax.ShapeDtypeStruct(position_scores.shape, f32),
+        ),
+        in_specs=[pl.BlockSpec(memory_space=pltpu.VMEM)] * 4,
+        out_specs=(pl.BlockSpec(memory_space=pltpu.VMEM),) * 2,
+        scratch_shapes=[pltpu.VMEM((chips,) + part, bf16)] * 3
+        + [pltpu.VMEM((chips,) + part_raw, f32)] * 3
+        + [
+            pltpu.SemaphoreType.DMA((2, 2 * chips)),
+            pltpu.SemaphoreType.DMA((2, 2 * chips)),
+        ],
+        compiler_params=pltpu.CompilerParams(
+            collective_id=1, has_side_effects=True, vmem_limit_bytes=VMEM_LIMIT
+        ),
+        name="scatter_rows",
+    )(parts, raw, grad_self, position_scores)
+
+
 def node_kernel(
-    items, aggregate, w_self, w_neighbor, bias, gain, queries, ids, cot,
-    hidden, grad_self, back_source, raw, weights, table, picks,
+    cols, steps, items, aggregate, w_self, w_neighbor, bias, gain, queries, ids, cot,
+    hidden, grad_self, source, raw,
+    grads, table, picks, send, recv,
 ):
-    weights_of(ids, cot, weights)
-    new, grad = node_math(
-        items[...], aggregate[...], w_self[...], w_neighbor[...], bias[...], gain[...],
-        weights[...], queries[...],
-    )
-    hidden[...] = new
-    last = ((1,), (1,))
-    back_source[...] = dot(grad, w_neighbor[...], last).astype(bf16)
-    grad_self[...] = dot(grad, w_self[...], last)
-    table[...] = dot(new, queries[...], last)
-    picked_scores(ids, table, picks, raw)
-
-
-def node_step(items, aggregate, w_self, w_neighbor, bias, gain, queries, ids, cot):
+    me = lax.axis_index("col")
+    rows = items.shape[0] // steps
+    width = items.shape[1]
+    ways = (1, -1)
+    is_inner = (me < cols - 1, me > 0)
+    barrier = pltpu.get_barrier_semaphore()
+    for way in range(2):
+
+        @pl.when(is_inner[way])
+        def _():
+            pl.semaphore_signal(
+                barrier, inc=1, device_id={"col": me + ways[way]},
+                device_id_type=pl.DeviceIdType.MESH,
+            )
+
+    pl.semaphore_wait(
+        barrier, is_inner[0].astype(jnp.int32) + is_inner[1].astype(jnp.int32)
+    )
+
+    def hop(way, far, j, piece):
+        ref = source.at[piece, pl.ds(j * rows, rows)]
+        return remote(
+            ref, ref, send.at[way, far, j], recv.at[way, far, j], {"col": me + ways[way]}
+        )
+
+    def outgoing(way, far, j):
+        return hop(way, far, j, me - ways[way] * far)
+
+    def incoming(way, far, j):
+        return hop(way, far, j, me - ways[way] * (far + 1))
+
+    def has(way, far):
+        return me >= far if way == 0 else me + far < cols
+
+    def node_part(j):
+        span = pl.ds(j * rows, rows)
+        weights = part_weights(ids, cot, j * rows, rows)
+        new, grad = node_math(
+            items[span, :], aggregate[span, :], w_self[...], w_neighbor[...], bias[...],
+            gain[...], weights, queries[...],
+        )
+        hidden[span, :] = new
+        grads[span, :] = grad
+        source[me, span, :] = dot(grad, w_neighbor[...], ((1,), (1,))).astype(bf16)
+        for way in range(2):
+
+            @pl.when(is_inner[way])
+            def _():
+                outgoing(way, 0, j).start()
+
+    def late_part(j):
+        span = pl.ds(j * rows, rows)
+        last = ((1,), (1,))
+        grad_self[span, :] = dot(grads[span, :], w_self[...], last)
+        table[...] = dot(hidden[span, :], queries[...], last)
+        part_scores(ids, table, j * rows, rows, picks)
+
+    picks[...] = jnp.zeros_like(picks)
+    for j in range(steps):
+        node_part(j)
+    for far in range(cols - 1):
+        for j in range(steps):
+            if far == 0:
+                late_part(j)
+            for way in range(2):
+
+                @pl.when(has(way, far + 1))
+                def _():
+                    incoming(way, far, j).wait_recv()
+
+                if far + 1 < cols - 1:
+
+                    @pl.when(has(way, far + 1) & is_inner[way])
+                    def _():
+                        outgoing(way, far + 1, j).start()
+
+    raw[...] = jnp.sum(picks[...], axis=1).T
+    for far in range(cols - 1):
+        for j in range(steps):
+            for way in range(2):
+
+                @pl.when(has(way, far) & is_inner[way])
+                def _():
+                    outgoing(way, far, j).wait_send()
+
+
+def part_weights(ids, cot, start, rows):
+    queries = ids.shape[1]
+    numbers = lax.broadcasted_iota(jnp.int32, (rows, queries), 0) + start
+    acc = jnp.zeros((rows, queries), f32)
+    for k in range(ids.shape[0]):
+        acc += jnp.where(numbers == ids[k : k + 1, :], cot[k : k + 1, :], 0.0)
+    return acc
+
+
+def part_scores(ids, table, start, rows, picks):
+    queries = ids.shape[1]
+    numbers = lax.broadcasted_iota(jnp.int32, (rows, queries), 0) + start
+    values = table[...]
+    for k in range(ids.shape[0]):
+        hit = jnp.where(numbers == ids[k : k + 1, :], values, 0.0)
+        picks[k] += jnp.sum(hit.reshape(rows // 8, 8, queries), axis=0)
+
+
+def node_step(cols, items, aggregate, w_self, w_neighbor, bias, gain, queries, ids, cot):
     rows, width = items.shape
     requests = queries.shape[0]
     cands = ids.shape[0]
+    steps = max(rows // 128, 1)
     return pl.pallas_call(
-        node_kernel,
+        functools.partial(node_kernel, cols, steps),
         out_shape=(
             jax.ShapeDtypeStruct((rows, width), bf16),
             jax.ShapeDtypeStruct((rows, width), f32),
-            jax.ShapeDtypeStruct((rows, width), bf16),
-            jax.ShapeDtypeStruct((cands, requests), f32),
-        ),
+            jax.ShapeDtypeStruct((cols, rows, width), bf16),
+            jax.ShapeDtypeStruct((requests, cands), f32),
+        ),
+        in_specs=[pl.BlockSpec(memory_space=pltpu.VMEM)] * 9,
+        out_specs=(pl.BlockSpec(memory_space=pltpu.VMEM),) * 4,
         scratch_shapes=[
-            pltpu.VMEM((rows, requests), f32),
-            pltpu.VMEM((rows, requests), f32),
+            pltpu.VMEM((rows, width), bf16),
+            pltpu.VMEM((rows // steps, requests), f32),
             pltpu.VMEM((cands, 8, requests), f32),
+            pltpu.SemaphoreType.DMA((2, cols, steps)),
+            pltpu.SemaphoreType.DMA((2, cols, steps)),
         ],
-        compiler_params=pltpu.CompilerParams(vmem_limit_bytes=VMEM_LIMIT),
+        compiler_params=pltpu.CompilerParams(
+            collective_id=2, has_side_effects=True, vmem_limit_bytes=VMEM_LIMIT
+        ),
         name="node_step",
     )(items, aggregate, w_self, w_neighbor, bias[None], gain[None], queries, ids, cot)
 
@@ -181,39 +414,42 @@
     cands = candidates.shape[1]
     col_count = lax.axis_size("col")
     row_count = lax.axis_size("row")
-    column_items = lax.all_gather(item_features, "row", axis=0, tiled=True)
     packed = jnp.concatenate(
         [queries.astype(f32), candidates.astype(f32), score_cotangent.astype(f32)], axis=1
     )
-    packed = lax.all_gather(packed, "row", axis=0, tiled=True)
+    column_items, packed = gather_rows(row_count, item_features, packed)
+    packed = packed.reshape(-1, width + 2 * cands)
     all_queries = packed[:, :width].astype(bf16)
     all_ids = packed[:, width : width + cands].astype(jnp.int32).T
     all_cot = packed[:, width + cands :].T
     my_piece = lax.axis_index("row") * col_count + lax.axis_index("col")
     local_ids = jnp.where(all_ids // rows_dev == my_piece, all_ids % rows_dev, -1)
+    tower_values = jnp.sum(jax.nn.relu(position_table) * tower_weight, axis=-1)
+    position_hits = positions[..., None] == jnp.arange(tower_values.shape[0])
+    position_scores = jnp.sum(jnp.where(position_hits, tower_values, 0.0), axis=-1)
 
     parts = block_products(
         tiles, block_rows[0, 0], block_cols[0, 0], counts[0],
         column_items, col_count * rows_dev // block, False,
     )
     aggregate = lax.psum_scatter(parts, "col", scatter_dimension=0, tiled=True)
-    hidden, grad_self, back_source, raw = node_step(
-        item_features, aggregate, self_weight, neighbor_weight, layer_bias, norm_gain,
-        all_queries, local_ids, all_cot,
-    )
-    range_source = lax.all_gather(back_source, "col", axis=0, tiled=True)
+    hidden, grad_self, range_source, raw = node_step(
+        col_count, item_features, aggregate, self_weight, neighbor_weight, layer_bias,
+        norm_gain, all_queries, local_ids, all_cot,
+    )
     back_parts = block_products(
         tiles, block_cols[0, 0], block_rows[0, 0], counts[0],
         range_source, row_count * rows_dev // block, True,
     )
-    raw_scores = lax.psum_scatter(raw.T, "row", scatter_dimension=0, tiled=True)
-    tower_values = jnp.sum(jax.nn.relu(position_table) * tower_weight, axis=-1)
-    position_hits = positions[..., None] == jnp.arange(tower_values.shape[0])
-    scores = raw_scores * width ** (-0.5) + jnp.sum(
-        jnp.where(position_hits, tower_values, 0.0), axis=-1
-    )
-    back_sum = lax.psum_scatter(back_parts, "row", scatter_dimension=0, tiled=True)
-    return (hidden, scores, grad_self + back_sum.astype(f32))
+    item_grads, scores = scatter_rows(
+        row_count,
+        back_parts.reshape(row_count, rows_dev, width),
+        raw.reshape(row_count, -1, cands),
+        grad_self,
+        position_scores,
+        width ** (-0.5),
+    )
+    return (hidden, scores, item_grads)
 
 
 def solution(mesh):

time: 209 us -> 151 us (0.72)
  waiting for transfers between devices: 140 us -> 23.4 us
  Pallas kernels: 32.2 us -> 101 us
  blocking collectives: 13.7 us -> 0 us
    reduce_scatter x2 -> x0, waiting for transfers between devices: 64.2 us -> none  [the longest x1 43.1 us: body(): lax.psum_scatter(back_parts, 'row', scatter_dimension=0, tiled=True)]
    all_gather x2 -> x0, waiting for transfers between devices: 57.1 us -> none  [the longest x1 31.9 us: body(): column_items = lax.all_gather(item_features, 'row', axis=0, tiled=True)]
    pallas_call x1 -> x3, Pallas kernels: 6.23 us -> 61 us  [the longest x1 23.4 us: node_step(): pl.pallas_call(functools.partial(node_kernel, cols, steps), out_shape=(ja...]
    pallas_call x2, Pallas kernels: 26 us -> 40.2 us  [block_products(): pl.pallas_call(functools.partial(block_kernel, transpose, chunk, 4), grid...]
    all_gather x1 -> x0, blocking collectives: 13.7 us -> none  [body(): packed = lax.all_gather(packed, 'row', axis=0, tiled=True)]
    reduce_scatter x1, waiting for transfers between devices: 17.6 us -> 23.4 us  [body(): aggregate = lax.psum_scatter(parts, 'col', scatter_dimension=0, tiled=True)]
    add x2 -> x0, other arithmetic: 3.09 us -> none  [the longest x1 1.79 us: body(): return (hidden, scores, grad_self + back_sum.astype(f32))]
    unnamed x17 -> x15, local copies, waits for them, and re-layouts: 2.97 us -> 4.68 us
  transfers between devices with their start and end apart: 5 -> 1, of which waited for: 5 -> 1; matrix products, arithmetic and copies ran while one was open for 3% -> 2% of each run, Pallas kernels for 6% -> 0%
where the time goes in v2:
time: 151 us; the launch traced here: 149 us
  Pallas kernels  101 us (67%)
  waiting for transfers between devices  23.4 us (15%)
  between operations  14.8 us (10%)
  local copies, waits for them, and re-layouts  5.39 us (4%)
  other arithmetic  4.52 us (3%)
    pallas_call x2, Pallas kernels, block_products(): pl.pallas_call(functools.partial(block_kernel, transpose, chunk, 4), grid...  40.2 us
    pallas_call x1, Pallas kernels, node_step(): pl.pallas_call(functools.partial(node_kernel, cols, steps), out_shape=(ja...  23.4 us
    reduce_scatter x1, waiting for transfers between devices, body(): aggregate = lax.psum_scatter(parts, 'col', scatter_dimension=0, tiled=True)  23.4 us
    pallas_call x1, Pallas kernels, gather_rows(): pl.pallas_call(functools.partial(gather_kernel, chips), out_shape=tuple((...  20.3 us
    pallas_call x1, Pallas kernels, scatter_rows(): pl.pallas_call(functools.partial(scatter_kernel, chips, scale), out_shape...  17.3 us
    unnamed x15, local copies, waits for them, and re-layouts  4.68 us
  transfers between devices with their start and end apart: 1, of which 1 were waited for; matrix products, arithmetic and copies ran while one was open for 2% of the time, Pallas kernels for 0%

profile of v2, /device:TPU:0, one launch (start us, length us, event | category | flops | bytes accessed | tf_op | source)
XLA Modules:
  0.0 149.4 jit_solution(15111264479539187918)
XLA Ops:
  7.2 0.0 reduce-scatter.2.cloned.1.call-start
  7.2 0.7 convert_element_type.13
  7.9 0.7 convert_element_type.14
  8.6 0.7 convert_element_type.15
  10.0 0.7 pad_maximum_fusion.refs_1_
  10.6 20.3 %gather_rows.1 = (bf16[8,512,256]{2,1,0:T(8,128)(2,1)}, f32[8,16,384]{2,1,0:T(8,128)}) custom-call(bf16[512,256]{1,0:T(8,128)(2,1)} %items.1, f32[16,384]{1,0:T(8,128)} %pad_maximum_fusion.refs_1_), custom_call_target="tpu_custom_call" | custom-call | tf_op jit(solution)/shard_map/gather_rows/pallas_call | solution.py:163
  30.9 0.0 copy-start.1
  30.9 0.0 copy-start.2
  31.0 0.0 copy-start.4
  31.0 0.0 copy-start.3
  31.0 18.9 %block_products.2 = bf16[16,128,256]{2,1,0:T(8,128)(2,1)} custom-call(s32[256]{0:T(256)} %bitcast.51, s32[256]{0:T(256)} %bitcast.53, s32[1]{0:T(128)} %bitcast.39.count, bf16[256,128,128]{2,1,0:T(8,128)(2,1)} %bitcast.41, bf16[32,128,256]{2,1,0:T(8,128)(2,1)} %bitcast.45), custom_call_target="tpu_custom_call" | custom-call | tf_op jit(solution)/shard_map/block_products/pallas_call | solution.py:53
  49.9 0.0 reduce-scatter.2.cloned.1.call-update
  49.9 0.0 copy-done.1
  49.9 0.6 slice.17.queries
  50.5 0.1 fusion.5
  50.6 0.1 copy.24
  50.7 0.7 copy.25
  51.4 0.0 copy-done.2
  51.4 0.0 copy-done.4
  51.4 0.1 multiply_reduce_fusion
  51.5 0.0 copy-done.3
  51.5 1.0 select_reduce_fusion.position_scores
  52.5 0.7 fusion.1.ids
  53.2 23.4 %reduce-scatter.2.cloned.1.call-done.aggregate = bf16[512,256]{1,0:T(8,128)(2,1)} async-done(((bf16[2048,256]{1,0:T(8,128)(2,1)}), bf16[512,256]{1,0:T(8,128)(2,1)}) %reduce-scatter.2.cloned.1.call-update) | async-done | bytes 262160 | tf_op jit(solution)/shard_map/reduce_scatter | solution.py:435
  76.6 23.4 %node_step.1 = (bf16[512,256]{1,0:T(8,128)(2,1)}, f32[512,256]{1,0:T(8,128)}, bf16[4,512,256]{2,1,0:T(8,128)(2,1)}, f32[128,64]{1,0:T(8,128)}) custom-call(bf16[512,256]{1,0:T(8,128)(2,1)} %items.1, bf16[512,256]{1,0:T(8,128)(2,1)} %reduce-scatter.2.cloned.1.call-done.aggregate, bf16[256,256]{1,0:T(8,128)(2,1)} %w_self.1, bf16[256,256]{1,0:T(8,128)(2,1)} %w_neighbor.1, ...), custom_call_target="tpu_custom_call" | custom-call | tf_op jit(solution)/shard_map/node_step/pallas_call | solution.py:370
  100.0 21.3 %block_products.3 = bf16[32,128,256]{2,1,0:T(8,128)(2,1)} custom-call(s32[256]{0:T(256)} %bitcast.54, s32[256]{0:T(256)} %bitcast.52, s32[1]{0:T(128)} %bitcast.40.count, bf16[256,128,128]{2,1,0:T(8,128)(2,1)} %bitcast.42, bf16[16,128,256]{2,1,0:T(8,128)(2,1)} %bitcast.46), custom_call_target="tpu_custom_call" | custom-call | tf_op jit(solution)/shard_map/block_products/pallas_call | solution.py:53
  121.3 0.0 copy-start
  121.3 17.3 %scatter_rows.1 = (f32[512,256]{1,0:T(8,128)}, f32[16,64]{1,0:T(8,128)}) custom-call(bf16[8,512,256]{2,1,0:T(8,128)(2,1)} %bitcast.43, f32[8,16,64]{2,1,0:T(8,128)} %bitcast.50, f32[512,256]{1,0:T(8,128)} %get-tuple-element.16.grad_self, f32[16,64]{1,0:T(8,128)} %select_reduce_fusion.position_scores), custom_call_target="tpu_custom_call" | custom-call | tf_op jit(solution)/shard_map/scatter_rows/pallas_call | solution.py:235
  138.7 0.0 copy-done
  138.7 0.7 copy.30
  139.4 1.3 copy.31
  140.7 1.9 %copy.32 = f32[512,256]{1,0:T(8,128)} copy(f32[512,256]{1,0:T(8,128)} %get-tuple-element.26) | data formatting | bytes 1048576
Async XLA Ops:
  7.2 69.4 %reduce-scatter.2.cloned.1.call-start = ((), (), s32[]{:S(2)}) async-start(), calls=%async_computation.1 | async-start | bytes 1310720 | tf_op jit(solution)/shard_map/reduce_scatter | solution.py:435
  30.9 19.0 %copy-start.1 = (f32[8,16,384]{2,1,0:T(8,128)S(1)}, f32[8,16,384]{2,1,0:T(8,128)}, u32[]{:S(2)}) copy-start(f32[8,16,384]{2,1,0:T(8,128)} %get-tuple-element.12) | copy-start | bytes 589828
  30.9 20.5 %copy-start.2 = (f32[64,128]{1,0:T(8,128)S(1)}, f32[64,128]{1,0:T(8,128)}, u32[]{:S(2)}) copy-start(f32[64,128]{1,0:T(8,128)} %param.27) | copy-start | bytes 98308
  31.0 20.5 %copy-start.4 = (f32[128]{0:T(128)S(1)}, f32[128]{0:T(128)}, u32[]{:S(2)}) copy-start(f32[128]{0:T(128)} %param.28) | copy-start | bytes 1540
  31.0 20.6 %copy-start.3 = (s32[16,64]{1,0:T(8,128)S(1)}, s32[16,64]{1,0:T(8,128)}, u32[]{:S(2)}) copy-start(s32[16,64]{1,0:T(8,128)} %param.26) | copy-start | bytes 12292
  121.3 17.3 %copy-start = (bf16[512,256]{1,0:T(8,128)(2,1)S(1)}, bf16[512,256]{1,0:T(8,128)(2,1)}, u32[]{:S(2)}) copy-start(bf16[512,256]{1,0:T(8,128)(2,1)} %get-tuple-element.24) | copy-start | bytes 786436
Sparse Core Ops, SparseCore 0:
  50.0 26.5 reduce-scatter.1

commit v3 on v2

--- a/solution.py
+++ b/solution.py
@@ -18,59 +18,80 @@
 
 
 def block_kernel(
-    transpose, chunk, unroll, targets, sources, count, tiles, source, out, total
+    transpose, chunk, unroll, targets, sources, count, tiles, source, *refs
 ):
-    step = pl.program_id(0)
+    kept = (len(refs) - 5) // 2
+    out = refs[kept]
+    total, held, held_source, arrived, source_arrived = refs[2 * kept + 1 :]
     target_blocks = out.shape[0]
-
-    @pl.when(step == 0)
-    def _():
-        total[...] = jnp.zeros_like(total)
-
-    live = jnp.clip(count[0] - step * chunk, 0, chunk)
+    chunks = tiles.shape[0] // chunk
+    live = count[0]
+
+    def fetch(index):
+        span = pl.ds(index * chunk, chunk)
+        return pltpu.make_async_copy(tiles.at[span], held.at[span], arrived.at[index])
+
+    fetch_source = pltpu.make_async_copy(source, held_source, source_arrived)
+    fetch_source.start()
+    for index in range(chunks):
+
+        @pl.when(index * chunk < live)
+        def _():
+            fetch(index).start()
+
+    total[...] = jnp.zeros_like(total)
+    for n in range(kept):
+        refs[kept + 1 + n][...] = refs[n][...]
+    fetch_source.wait()
 
     def group(index, carry):
         for lane in range(unroll):
-            slot = index * unroll + lane
-            place = step * chunk + slot
-            target = jnp.where(slot < live, targets[place], target_blocks)
+            place = index * unroll + lane
+            target = jnp.where(place < live, targets[place], target_blocks)
             dims = ((0,), (0,)) if transpose else ((1,), (0,))
-            total[target] += dot(tiles[slot], source[sources[place]], dims)
+            total[target] += dot(held[place], held_source[sources[place]], dims)
         return carry
 
-    lax.fori_loop(0, (live + unroll - 1) // unroll, group, 0)
-
-    @pl.when(step == pl.num_programs(0) - 1)
-    def _():
-        out[...] = total[0:target_blocks].astype(out.dtype)
-
-
-def block_products(tiles, targets, sources, count, source, target_blocks, transpose):
+    def part(index, carry):
+        fetch(index).wait()
+        start = index * (chunk // unroll)
+        stop = jnp.minimum(start + chunk // unroll, (live + unroll - 1) // unroll)
+        return lax.fori_loop(start, stop, group, carry)
+
+    lax.fori_loop(0, (live + chunk - 1) // chunk, part, 0)
+    out[...] = total[0:target_blocks].astype(out.dtype)
+
+
+def block_products(tiles, targets, sources, count, source, target_blocks, transpose, kept=()):
     slots, block, _ = tiles.shape
     width = source.shape[-1]
-    chunk = min(32, slots)
+    chunk = min(16, slots)
     shaped = source.reshape(-1, block, width)
-    return pl.pallas_call(
-        functools.partial(block_kernel, transpose, chunk, 4),
-        grid_spec=pltpu.PrefetchScalarGridSpec(
-            num_scalar_prefetch=3,
-            grid=(slots // chunk,),
-            in_specs=[
-                pl.BlockSpec((chunk, block, block), lambda i, *_: (i, 0, 0)),
-                pl.BlockSpec(shaped.shape, lambda i, *_: (0, 0, 0)),
-            ],
-            out_specs=pl.BlockSpec((target_blocks, block, width), lambda i, *_: (0, 0, 0)),
-            scratch_shapes=[pltpu.VMEM((target_blocks + 1, block, width), f32)],
-        ),
-        out_shape=jax.ShapeDtypeStruct((target_blocks, block, width), bf16),
+    whole = pl.BlockSpec(memory_space=pltpu.VMEM)
+    scalars = pl.BlockSpec(memory_space=pltpu.SMEM)
+    stays = pl.BlockSpec(memory_space=pl.ANY)
+    out, *rest = pl.pallas_call(
+        functools.partial(block_kernel, transpose, chunk, min(8, chunk)),
+        in_specs=[scalars] * 3 + [stays] * 2 + [whole] * len(kept),
+        out_specs=(whole,) * (1 + len(kept)),
+        scratch_shapes=[
+            pltpu.VMEM((target_blocks + 1, block, width), f32),
+            pltpu.VMEM(tiles.shape, bf16),
+            pltpu.VMEM(shaped.shape, bf16),
+            pltpu.SemaphoreType.DMA((slots // chunk,)),
+            pltpu.SemaphoreType.DMA,
+        ],
+        out_shape=(jax.ShapeDtypeStruct((target_blocks, block, width), bf16),)
+        + tuple(jax.ShapeDtypeStruct(array.shape, array.dtype) for array in kept),
         compiler_params=pltpu.CompilerParams(vmem_limit_bytes=VMEM_LIMIT),
         name="block_products",
-    )(targets, sources, count, tiles, shaped).reshape(target_blocks * block, width)
-
-
-def node_math(items, aggregate, w_self, w_neighbor, bias, gain, weights, queries):
-    width = items.shape[1]
-    preact = dot(items, w_self) + dot(aggregate.astype(bf16), w_neighbor) + bias
+    )(targets, sources, count, tiles, shaped, *kept)
+    return (out.reshape(target_blocks * block, width), *rest)
+
+
+def node_math(base, aggregate, w_neighbor, gain, weights, queries):
+    width = base.shape[1]
+    preact = base + dot(aggregate.astype(bf16), w_neighbor)
     gate = 1.0 / (1.0 + jnp.exp(-preact))
     active = preact * gate
     scale = lax.rsqrt(jnp.mean(active * active, axis=-1, keepdims=True) + norm_eps)
@@ -110,13 +131,17 @@
     return me, core, ahead, behind
 
 
-def gather_kernel(chips, *refs):
-    arrays = len(refs) // 2 - 1
-    inputs, outputs = refs[:arrays], refs[arrays : 2 * arrays]
-    send, recv = refs[2 * arrays :]
+def gather_kernel(
+    chips, items, queries, candidates, cotangent, all_items, all_packed, packed, send, recv
+):
+    arrays = 2
+    inputs, outputs = (items, packed), (all_items, all_packed)
     me, core, ahead, behind = row_places(chips)
     sibling = {"row": me + 1 - 2 * core}
     peers = [{"row": ahead[i] * 2 + core} for i in range(chips)]
+    packed[...] = jnp.concatenate(
+        [ref[...].astype(f32) for ref in (queries, candidates, cotangent)], axis=1
+    )
     greet(peers[1:] + [sibling])
     copies = []
     for n in range(arrays):
@@ -158,24 +183,29 @@
         copy.wait()
 
 
-def gather_rows(row_count, *arrays):
+def gather_rows(row_count, items, queries, candidates, cotangent):
     chips = row_count // 2
+    small = (queries, candidates, cotangent)
+    packed = (queries.shape[0], sum(array.shape[1] for array in small))
     return pl.pallas_call(
         functools.partial(gather_kernel, chips),
-        out_shape=tuple(
-            jax.ShapeDtypeStruct((row_count,) + array.shape, array.dtype) for array in arrays
+        out_shape=(
+            jax.ShapeDtypeStruct((row_count,) + items.shape, items.dtype),
+            jax.ShapeDtypeStruct((row_count,) + packed, f32),
         ),
-        in_specs=[pl.BlockSpec(memory_space=pl.ANY)] * len(arrays),
-        out_specs=tuple(pl.BlockSpec(memory_space=pl.ANY) for _ in arrays),
+        in_specs=[pl.BlockSpec(memory_space=pl.ANY)]
+        + [pl.BlockSpec(memory_space=pltpu.VMEM)] * 3,
+        out_specs=(pl.BlockSpec(memory_space=pl.ANY),) * 2,
         scratch_shapes=[
-            pltpu.SemaphoreType.DMA((len(arrays), 2 * chips)),
-            pltpu.SemaphoreType.DMA((len(arrays), 2 * chips)),
+            pltpu.VMEM(packed, f32),
+            pltpu.SemaphoreType.DMA((2, 2 * chips)),
+            pltpu.SemaphoreType.DMA((2, 2 * chips)),
         ],
         compiler_params=pltpu.CompilerParams(
             collective_id=0, has_side_effects=True, vmem_limit_bytes=VMEM_LIMIT
         ),
         name="gather_rows",
-    )(*arrays)
+    )(items, *small)
 
 
 def scatter_kernel(
@@ -254,11 +284,15 @@
 
 
 def node_kernel(
-    cols, steps, items, aggregate, w_self, w_neighbor, bias, gain, queries, ids, cot,
+    cols, steps, items, parts, w_self, w_neighbor, bias, gain, packed,
     hidden, grad_self, source, raw,
-    grads, table, picks, send, recv,
+    grads, table, picks, queries, ids, cot, weights, base, aggregate, inbox, outbox,
+    send, recv, sum_send, sum_recv,
 ):
     me = lax.axis_index("col")
+    piece = lax.axis_index("row") * cols + me
+    first_item = piece * items.shape[0]
+    cands = ids.shape[0]
     rows = items.shape[0] // steps
     width = items.shape[1]
     ways = (1, -1)
@@ -292,12 +326,58 @@
     def has(way, far):
         return me >= far if way == 0 else me + far < cols
 
+    def sum_hop(way, dest, j, ref):
+        return remote(
+            ref.at[pl.ds(j * rows, rows)], inbox.at[way, dest, pl.ds(j * rows, rows)],
+            sum_send.at[way, dest, j], sum_recv.at[way, dest, j], {"col": me + ways[way]},
+        )
+
+    def is_before(way, dest):
+        return me < dest if way == 0 else me > dest
+
+    def sum_part(way, dest, j):
+        span = pl.ds(j * rows, rows)
+        is_end = me == (0 if way == 0 else cols - 1)
+
+        @pl.when(is_end)
+        def _():
+            sum_hop(way, dest, j, parts.at[dest]).start()
+
+        @pl.when(is_before(way, dest) & jnp.logical_not(is_end))
+        def _():
+            sum_hop(way, dest, j, parts.at[dest]).wait_recv()
+            outbox[way, dest, span, :] = (
+                parts[dest, span, :].astype(f32) + inbox[way, dest, span, :].astype(f32)
+            ).astype(bf16)
+            sum_hop(way, dest, j, outbox.at[way, dest]).start()
+
+    for t in range(cols - 1):
+        for j in range(steps):
+            sum_part(0, cols - 1 - t, j)
+            sum_part(1, t, j)
+
+    queries[...] = packed[:, :width].astype(bf16)
+    tail = packed[:, width:].T
+    ids[...] = tail[:cands]
+    cot[...] = tail[cands:]
+    for j in range(steps):
+        span = pl.ds(j * rows, rows)
+        weights[span, :] = part_weights(ids, cot, first_item + j * rows, rows)
+        base[span, :] = dot(items[span, :], w_self[...]) + bias[...]
+
     def node_part(j):
         span = pl.ds(j * rows, rows)
-        weights = part_weights(ids, cot, j * rows, rows)
+        aggregate[...] = parts[me, span, :].astype(f32)
+        for way in range(2):
+
+            @pl.when(is_inner[1 - way])
+            def _():
+                sum_hop(way, me, j, parts.at[me]).wait_recv()
+                aggregate[...] += inbox[way, me, span, :].astype(f32)
+
         new, grad = node_math(
-            items[span, :], aggregate[span, :], w_self[...], w_neighbor[...], bias[...],
-            gain[...], weights, queries[...],
+            base[span, :], aggregate[...], w_neighbor[...], gain[...], weights[span, :],
+            queries[...],
         )
         hidden[span, :] = new
         grads[span, :] = grad
@@ -313,7 +393,7 @@
         last = ((1,), (1,))
         grad_self[span, :] = dot(grads[span, :], w_self[...], last)
         table[...] = dot(hidden[span, :], queries[...], last)
-        part_scores(ids, table, j * rows, rows, picks)
+        part_scores(ids, table, first_item + j * rows, rows, picks)
 
     picks[...] = jnp.zeros_like(picks)
     for j in range(steps):
@@ -343,10 +423,18 @@
                 def _():
                     outgoing(way, far, j).wait_send()
 
+    for dest in range(cols):
+        for j in range(steps):
+            for way in range(2):
+
+                @pl.when(is_before(way, dest))
+                def _():
+                    sum_hop(way, dest, j, parts.at[dest]).wait_send()
+
 
 def part_weights(ids, cot, start, rows):
     queries = ids.shape[1]
-    numbers = lax.broadcasted_iota(jnp.int32, (rows, queries), 0) + start
+    numbers = (lax.broadcasted_iota(jnp.int32, (rows, queries), 0) + start).astype(f32)
     acc = jnp.zeros((rows, queries), f32)
     for k in range(ids.shape[0]):
         acc += jnp.where(numbers == ids[k : k + 1, :], cot[k : k + 1, :], 0.0)
@@ -355,18 +443,18 @@
 
 def part_scores(ids, table, start, rows, picks):
     queries = ids.shape[1]
-    numbers = lax.broadcasted_iota(jnp.int32, (rows, queries), 0) + start
+    numbers = (lax.broadcasted_iota(jnp.int32, (rows, queries), 0) + start).astype(f32)
     values = table[...]
     for k in range(ids.shape[0]):
         hit = jnp.where(numbers == ids[k : k + 1, :], values, 0.0)
         picks[k] += jnp.sum(hit.reshape(rows // 8, 8, queries), axis=0)
 
 
-def node_step(cols, items, aggregate, w_self, w_neighbor, bias, gain, queries, ids, cot):
+def node_step(cols, items, parts, w_self, w_neighbor, bias, gain, packed, cands):
     rows, width = items.shape
-    requests = queries.shape[0]
-    cands = ids.shape[0]
+    requests = packed.shape[0]
     steps = max(rows // 128, 1)
+    moves = pltpu.SemaphoreType.DMA((2, cols, steps))
     return pl.pallas_call(
         functools.partial(node_kernel, cols, steps),
         out_shape=(
@@ -375,20 +463,30 @@
             jax.ShapeDtypeStruct((cols, rows, width), bf16),
             jax.ShapeDtypeStruct((requests, cands), f32),
         ),
-        in_specs=[pl.BlockSpec(memory_space=pltpu.VMEM)] * 9,
+        in_specs=[pl.BlockSpec(memory_space=pltpu.VMEM)] * 7,
         out_specs=(pl.BlockSpec(memory_space=pltpu.VMEM),) * 4,
         scratch_shapes=[
             pltpu.VMEM((rows, width), bf16),
             pltpu.VMEM((rows // steps, requests), f32),
             pltpu.VMEM((cands, 8, requests), f32),
-            pltpu.SemaphoreType.DMA((2, cols, steps)),
-            pltpu.SemaphoreType.DMA((2, cols, steps)),
+            pltpu.VMEM((requests, width), bf16),
+            pltpu.VMEM((cands, requests), f32),
+            pltpu.VMEM((cands, requests), f32),
+            pltpu.VMEM((rows, requests), f32),
+            pltpu.VMEM((rows, width), f32),
+            pltpu.VMEM((rows // steps, width), f32),
+            pltpu.VMEM((2, cols, rows, width), bf16),
+            pltpu.VMEM((2, cols, rows, width), bf16),
+            moves,
+            moves,
+            moves,
+            moves,
         ],
         compiler_params=pltpu.CompilerParams(
             collective_id=2, has_side_effects=True, vmem_limit_bytes=VMEM_LIMIT
         ),
         name="node_step",
-    )(items, aggregate, w_self, w_neighbor, bias[None], gain[None], queries, ids, cot)
+    )(items, parts, w_self, w_neighbor, bias[None], gain[None], packed)
 
 
 def body(
@@ -414,32 +512,24 @@
     cands = candidates.shape[1]
     col_count = lax.axis_size("col")
     row_count = lax.axis_size("row")
-    packed = jnp.concatenate(
-        [queries.astype(f32), candidates.astype(f32), score_cotangent.astype(f32)], axis=1
-    )
-    column_items, packed = gather_rows(row_count, item_features, packed)
-    packed = packed.reshape(-1, width + 2 * cands)
-    all_queries = packed[:, :width].astype(bf16)
-    all_ids = packed[:, width : width + cands].astype(jnp.int32).T
-    all_cot = packed[:, width + cands :].T
-    my_piece = lax.axis_index("row") * col_count + lax.axis_index("col")
-    local_ids = jnp.where(all_ids // rows_dev == my_piece, all_ids % rows_dev, -1)
+    column_items, packed = gather_rows(
+        row_count, item_features, queries, candidates, score_cotangent
+    )
     tower_values = jnp.sum(jax.nn.relu(position_table) * tower_weight, axis=-1)
     position_hits = positions[..., None] == jnp.arange(tower_values.shape[0])
     position_scores = jnp.sum(jnp.where(position_hits, tower_values, 0.0), axis=-1)
 
-    parts = block_products(
+    (parts,) = block_products(
         tiles, block_rows[0, 0], block_cols[0, 0], counts[0],
         column_items, col_count * rows_dev // block, False,
     )
-    aggregate = lax.psum_scatter(parts, "col", scatter_dimension=0, tiled=True)
     hidden, grad_self, range_source, raw = node_step(
-        col_count, item_features, aggregate, self_weight, neighbor_weight, layer_bias,
-        norm_gain, all_queries, local_ids, all_cot,
-    )
-    back_parts = block_products(
+        col_count, item_features, parts.reshape(col_count, rows_dev, width), self_weight,
+        neighbor_weight, layer_bias, norm_gain, packed.reshape(-1, packed.shape[-1]), cands,
+    )
+    back_parts, hidden = block_products(
         tiles, block_cols[0, 0], block_rows[0, 0], counts[0],
-        range_source, row_count * rows_dev // block, True,
+        range_source, row_count * rows_dev // block, True, (hidden,),
     )
     item_grads, scores = scatter_rows(
         row_count,

time: 151 us -> 132 us (0.87)
  Pallas kernels: 101 us -> 125 us
  waiting for transfers between devices: 23.4 us -> 0 us
  between operations: 14.8 us -> 1.37 us
  other arithmetic: 4.52 us -> 1.1 us
  local copies, waits for them, and re-layouts: 5.39 us -> 3.18 us
    pallas_call x1, Pallas kernels: 23.4 us -> 53.9 us  [node_step(): pl.pallas_call(functools.partial(node_kernel, cols, steps), out_shape=(ja...]
    reduce_scatter x1 -> x0, waiting for transfers between devices: 23.4 us -> none  [body(): aggregate = lax.psum_scatter(parts, 'col', scatter_dimension=0, tiled=True)]
    pallas_call x3, Pallas kernels: 60.5 us -> 54 us  [the longest x2 32.9 us: block_products(): pl.pallas_call(functools.partial(block_kernel, transpose, chunk, min(8, c...]
    convert_element_type x3 -> x0, other arithmetic: 2.09 us -> none  [the longest x1 0.7 us: body(): queries.astype(f32)]
    unnamed x15 -> x8, local copies, waits for them, and re-layouts: 4.68 us -> 3.18 us
  transfers between devices with their start and end apart: 1 -> 0, of which waited for: 1 -> 0; matrix products, arithmetic and copies ran while one was open for 2% -> 0% of each run, Pallas kernels for 0% -> 0%
where the time goes in v3:
time: 132 us; the launch traced here: 131 us
  Pallas kernels  125 us (95%)
  local copies, waits for them, and re-layouts  3.18 us (2%)
  between operations  1.37 us (1%)
    pallas_call x1, Pallas kernels, node_step(): pl.pallas_call(functools.partial(node_kernel, cols, steps), out_shape=(ja...  53.9 us
    pallas_call x2, Pallas kernels, block_products(): pl.pallas_call(functools.partial(block_kernel, transpose, chunk, min(8, c...  32.9 us
    pallas_call x1, Pallas kernels, gather_rows(): pl.pallas_call(functools.partial(gather_kernel, chips), out_shape=(jax.Sh...  21.1 us
    pallas_call x1, Pallas kernels, scatter_rows(): pl.pallas_call(functools.partial(scatter_kernel, chips, scale), out_shape...  17.3 us
    unnamed x8, local copies, waits for them, and re-layouts  3.18 us

profile of v3, /device:TPU:0, one launch (start us, length us, event | category | flops | bytes accessed | tf_op | source)
XLA Modules:
  0.0 130.8 jit_solution(15456499297814015137)
XLA Ops:
  0.6 21.1 %gather_rows.1 = (bf16[8,512,256]{2,1,0:T(8,128)(2,1)}, f32[8,16,384]{2,1,0:T(8,128)}) custom-call(bf16[512,256]{1,0:T(8,128)(2,1)} %items.3, bf16[16,256]{1,0:T(8,128)(2,1)} %queries.1, s32[16,64]{1,0:T(8,128)} %candidates.1, bf16[16,64]{1,0:T(8,128)(2,1)} %cotangent.1), custom_call_target="tpu_custom_call" | custom-call | tf_op jit(solution)/shard_map/gather_rows/pallas_call | solution.py:190
  22.4 15.6 %block_products.2 = bf16[16,128,256]{2,1,0:T(8,128)(2,1)} custom-call(s32[256]{0:T(256)} %bitcast.24, s32[256]{0:T(256)} %bitcast.22, s32[1]{0:T(128)} %bitcast.12.count, bf16[256,128,128]{2,1,0:T(8,128)(2,1)} %bitcast.14, bf16[32,128,256]{2,1,0:T(8,128)(2,1)} %bitcast.17), custom_call_target="tpu_custom_call" | custom-call | tf_op jit(solution)/shard_map/block_products/pallas_call | solution.py:73
  38.0 53.9 %node_step.1 = (bf16[512,256]{1,0:T(8,128)(2,1)}, f32[512,256]{1,0:T(8,128)}, bf16[4,512,256]{2,1,0:T(8,128)(2,1)}, f32[128,64]{1,0:T(8,128)}) custom-call(bf16[512,256]{1,0:T(8,128)(2,1)} %items.3, bf16[4,512,256]{2,1,0:T(8,128)(2,1)} %bitcast.16, bf16[256,256]{1,0:T(8,128)(2,1)} %w_self.1, bf16[256,256]{1,0:T(8,128)(2,1)} %w_neighbor.1, ...), custom_call_target="tpu_custom_call" | custom-call | tf_op jit(solution)/shard_map/node_step/pallas_call | solution.py:458
  91.9 0.0 copy-start
  91.9 0.0 copy-start.2
  92.0 0.0 copy-start.1
  92.0 17.2 %block_products.3 = (bf16[32,128,256]{2,1,0:T(8,128)(2,1)}, bf16[512,256]{1,0:T(8,128)(2,1)}) custom-call(s32[256]{0:T(256)} %bitcast.23, s32[256]{0:T(256)} %bitcast.25, s32[1]{0:T(128)} %bitcast.13.count, bf16[256,128,128]{2,1,0:T(8,128)(2,1)} %bitcast.15, bf16[16,128,256]{2,1,0:T(8,128)(2,1)} %bitcast.19, bf16[512,256]{1,0:T(8,128)(2,1)} %get-tuple-element.16.refs_0_), custom_call_target="tpu_custom_call" | custom-call | tf_op jit(solution)/shard_map/block_products/pallas_call | solution.py:73
  109.2 0.0 copy-done
  109.2 0.0 copy-done.2
  109.2 0.1 multiply_reduce_fusion
  109.3 0.0 copy-done.1
  109.3 1.0 select_reduce_fusion.position_scores
  110.3 17.3 %scatter_rows.1 = (f32[512,256]{1,0:T(8,128)}, f32[16,64]{1,0:T(8,128)}) custom-call(bf16[8,512,256]{2,1,0:T(8,128)(2,1)} %bitcast.18, f32[8,16,64]{2,1,0:T(8,128)} %bitcast.21, f32[512,256]{1,0:T(8,128)} %get-tuple-element.20.grad_self, f32[16,64]{1,0:T(8,128)} %select_reduce_fusion.position_scores), custom_call_target="tpu_custom_call" | custom-call | tf_op jit(solution)/shard_map/scatter_rows/pallas_call | solution.py:265
  127.6 1.3 copy.21
  128.9 1.9 %copy.22 = f32[512,256]{1,0:T(8,128)} copy(f32[512,256]{1,0:T(8,128)} %get-tuple-element.28) | data formatting | bytes 1048576
Async XLA Ops:
  91.9 17.3 %copy-start = (f32[64,128]{1,0:T(8,128)S(1)}, f32[64,128]{1,0:T(8,128)}, u32[]{:S(2)}) copy-start(f32[64,128]{1,0:T(8,128)} %param.27) | copy-start | bytes 98308
  91.9 17.3 %copy-start.2 = (f32[128]{0:T(128)S(1)}, f32[128]{0:T(128)}, u32[]{:S(2)}) copy-start(f32[128]{0:T(128)} %param.28) | copy-start | bytes 1540
  92.0 17.4 %copy-start.1 = (s32[16,64]{1,0:T(8,128)S(1)}, s32[16,64]{1,0:T(8,128)}, u32[]{:S(2)}) copy-start(s32[16,64]{1,0:T(8,128)} %param.26) | copy-start | bytes 12292

commit v4 on v3

--- a/solution.py
+++ b/solution.py
@@ -20,9 +20,10 @@
 def block_kernel(
     transpose, chunk, unroll, targets, sources, count, tiles, source, *refs
 ):
-    kept = (len(refs) - 5) // 2
+    kept = (len(refs) - 6) // 2
     out = refs[kept]
-    total, held, held_source, arrived, source_arrived = refs[2 * kept + 1 :]
+    even, odd, held, held_source, arrived, source_arrived = refs[2 * kept + 1 :]
+    totals = (even, odd)
     target_blocks = out.shape[0]
     chunks = tiles.shape[0] // chunk
     live = count[0]
@@ -39,17 +40,19 @@
         def _():
             fetch(index).start()
 
-    total[...] = jnp.zeros_like(total)
+    for total in totals:
+        total[...] = jnp.zeros_like(total)
     for n in range(kept):
         refs[kept + 1 + n][...] = refs[n][...]
     fetch_source.wait()
 
     def group(index, carry):
+        dims = ((0,), (0,)) if transpose else ((1,), (0,))
         for lane in range(unroll):
             place = index * unroll + lane
             target = jnp.where(place < live, targets[place], target_blocks)
-            dims = ((0,), (0,)) if transpose else ((1,), (0,))
-            total[target] += dot(held[place], held_source[sources[place]], dims)
+            product = dot(held[place], held_source[sources[place]], dims)
+            totals[lane % 2][target] += product
         return carry
 
     def part(index, carry):
@@ -59,7 +62,7 @@
         return lax.fori_loop(start, stop, group, carry)
 
     lax.fori_loop(0, (live + chunk - 1) // chunk, part, 0)
-    out[...] = total[0:target_blocks].astype(out.dtype)
+    out[...] = (even[0:target_blocks] + odd[0:target_blocks]).astype(out.dtype)
 
 
 def block_products(tiles, targets, sources, count, source, target_blocks, transpose, kept=()):
@@ -75,6 +78,7 @@
         in_specs=[scalars] * 3 + [stays] * 2 + [whole] * len(kept),
         out_specs=(whole,) * (1 + len(kept)),
         scratch_shapes=[
+            pltpu.VMEM((target_blocks + 1, block, width), f32),
             pltpu.VMEM((target_blocks + 1, block, width), f32),
             pltpu.VMEM(tiles.shape, bf16),
             pltpu.VMEM(shaped.shape, bf16),
@@ -221,14 +225,18 @@
     first = {}
     for i in order:
         for n, (mine, inbox, _, _) in enumerate(arrays):
-            copy = remote(
+            first[n, i] = remote(
                 mine.at[ahead[i] * 2 + 1 - core], inbox.at[i],
                 send.at[n, i], recv.at[n, i], sibling,
             )
-            copy.start()
-            first[n, i] = copy
+    for i in order:
+        first[1, i].start()
+    first[0, order[0]].start()
     second = []
-    for i in order:
+    for turn, i in enumerate(order):
+        first[0, i].wait_send()
+        if turn + 1 < chips:
+            first[0, order[turn + 1]].start()
         for n, (mine, inbox, summed, outbox) in enumerate(arrays):
             first[n, i].wait_recv()
             value = mine[ahead[i] * 2 + core].astype(f32) + inbox[i].astype(f32)
@@ -252,8 +260,8 @@
         else:
             scores[...] += far_raw[i]
     scores[...] = scores[...] * scale + position_scores[...]
-    for copy in first.values():
-        copy.wait_send()
+    for i in order:
+        first[1, i].wait_send()
     for _, _, copy in second:
         copy.wait_send()
 
@@ -335,12 +343,23 @@
     def is_before(way, dest):
         return me < dest if way == 0 else me > dest
 
-    def sum_part(way, dest, j):
+    in_flight = 3
+    turns = (cols - 1) * steps
+    order = (
+        [(cols - 1 - turn // steps, turn % steps) for turn in range(turns)],
+        [(turn // steps, turn % steps) for turn in range(turns)],
+    )
+
+    def sum_part(way, turn):
+        dest, j = order[way][turn]
         span = pl.ds(j * rows, rows)
         is_end = me == (0 if way == 0 else cols - 1)
 
         @pl.when(is_end)
         def _():
+            if turn >= in_flight:
+                old = order[way][turn - in_flight]
+                sum_hop(way, *old, parts.at[old[0]]).wait_send()
             sum_hop(way, dest, j, parts.at[dest]).start()
 
         @pl.when(is_before(way, dest) & jnp.logical_not(is_end))
@@ -351,10 +370,9 @@
             ).astype(bf16)
             sum_hop(way, dest, j, outbox.at[way, dest]).start()
 
-    for t in range(cols - 1):
-        for j in range(steps):
-            sum_part(0, cols - 1 - t, j)
-            sum_part(1, t, j)
+    for turn in range(turns):
+        sum_part(0, turn)
+        sum_part(1, turn)
 
     queries[...] = packed[:, :width].astype(bf16)
     tail = packed[:, width:].T
@@ -423,13 +441,16 @@
                 def _():
                     outgoing(way, far, j).wait_send()
 
-    for dest in range(cols):
-        for j in range(steps):
-            for way in range(2):
-
-                @pl.when(is_before(way, dest))
-                def _():
-                    sum_hop(way, dest, j, parts.at[dest]).wait_send()
+    for turn in range(turns):
+        for way in range(2):
+            dest, j = order[way][turn]
+            is_left = is_before(way, dest)
+            if turn < turns - in_flight:
+                is_left &= me != (0 if way == 0 else cols - 1)
+
+            @pl.when(is_left)
+            def _():
+                sum_hop(way, dest, j, parts.at[dest]).wait_send()
 
 
 def part_weights(ids, cot, start, rows):

time: 132 us -> 129 us (0.977)
  Pallas kernels: 125 us -> 123 us
    pallas_call x2, Pallas kernels: 32.9 us -> 14 us  [block_products(): pl.pallas_call(functools.partial(block_kernel, transpose, chunk, min(8, c...]
    pallas_call x1, Pallas kernels: 17.3 us -> 30.8 us  [scatter_rows(): pl.pallas_call(functools.partial(scatter_kernel, chips, scale), out_shape...]
    pallas_call x1, Pallas kernels: 53.9 us -> 56.7 us  [node_step(): pl.pallas_call(functools.partial(node_kernel, cols, steps), out_shape=(ja...]
where the time goes in v4:
time: 129 us; the launch traced here: 128 us
  Pallas kernels  123 us (95%)
  local copies, waits for them, and re-layouts  3.18 us (2%)
  between operations  1.37 us (1%)
    pallas_call x1, Pallas kernels, node_step(): pl.pallas_call(functools.partial(node_kernel, cols, steps), out_shape=(ja...  56.7 us
    pallas_call x1, Pallas kernels, scatter_rows(): pl.pallas_call(functools.partial(scatter_kernel, chips, scale), out_shape...  30.8 us
    pallas_call x1, Pallas kernels, gather_rows(): pl.pallas_call(functools.partial(gather_kernel, chips), out_shape=(jax.Sh...  21.1 us
    pallas_call x2, Pallas kernels, block_products(): pl.pallas_call(functools.partial(block_kernel, transpose, chunk, min(8, c...  14 us
    unnamed x8, local copies, waits for them, and re-layouts  3.18 us

profile of v4, /device:TPU:0, one launch (start us, length us, event | category | flops | bytes accessed | tf_op | source)
XLA Modules:
  0.0 128.2 jit_solution(532466062685762842)
XLA Ops:
  0.6 21.1 %gather_rows.1 = (bf16[8,512,256]{2,1,0:T(8,128)(2,1)}, f32[8,16,384]{2,1,0:T(8,128)}) custom-call(bf16[512,256]{1,0:T(8,128)(2,1)} %items.3, bf16[16,256]{1,0:T(8,128)(2,1)} %queries.1, s32[16,64]{1,0:T(8,128)} %candidates.1, bf16[16,64]{1,0:T(8,128)(2,1)} %cotangent.1), custom_call_target="tpu_custom_call" | custom-call | tf_op jit(solution)/shard_map/gather_rows/pallas_call | solution.py:194
  22.4 6.6 %block_products.2 = bf16[16,128,256]{2,1,0:T(8,128)(2,1)} custom-call(s32[256]{0:T(256)} %bitcast.24, s32[256]{0:T(256)} %bitcast.22, s32[1]{0:T(128)} %bitcast.12.count, bf16[256,128,128]{2,1,0:T(8,128)(2,1)} %bitcast.14, bf16[32,128,256]{2,1,0:T(8,128)(2,1)} %bitcast.17), custom_call_target="tpu_custom_call" | custom-call | tf_op jit(solution)/shard_map/block_products/pallas_call | solution.py:76
  29.0 56.7 %node_step.1 = (bf16[512,256]{1,0:T(8,128)(2,1)}, f32[512,256]{1,0:T(8,128)}, bf16[4,512,256]{2,1,0:T(8,128)(2,1)}, f32[128,64]{1,0:T(8,128)}) custom-call(bf16[512,256]{1,0:T(8,128)(2,1)} %items.3, bf16[4,512,256]{2,1,0:T(8,128)(2,1)} %bitcast.16, bf16[256,256]{1,0:T(8,128)(2,1)} %w_self.1, bf16[256,256]{1,0:T(8,128)(2,1)} %w_neighbor.1, ...), custom_call_target="tpu_custom_call" | custom-call | tf_op jit(solution)/shard_map/node_step/pallas_call | solution.py:479
  85.7 0.0 copy-start
  85.7 0.0 copy-start.2
  85.7 0.0 copy-start.1
  85.7 7.4 %block_products.3 = (bf16[32,128,256]{2,1,0:T(8,128)(2,1)}, bf16[512,256]{1,0:T(8,128)(2,1)}) custom-call(s32[256]{0:T(256)} %bitcast.23, s32[256]{0:T(256)} %bitcast.25, s32[1]{0:T(128)} %bitcast.13.count, bf16[256,128,128]{2,1,0:T(8,128)(2,1)} %bitcast.15, bf16[16,128,256]{2,1,0:T(8,128)(2,1)} %bitcast.19, bf16[512,256]{1,0:T(8,128)(2,1)} %get-tuple-element.16.refs_0_), custom_call_target="tpu_custom_call" | custom-call | tf_op jit(solution)/shard_map/block_products/pallas_call | solution.py:76
  93.1 0.0 copy-done
  93.1 0.0 copy-done.2
  93.1 0.1 multiply_reduce_fusion
  93.2 0.0 copy-done.1
  93.2 1.0 select_reduce_fusion.position_scores
  94.2 30.8 %scatter_rows.1 = (f32[512,256]{1,0:T(8,128)}, f32[16,64]{1,0:T(8,128)}) custom-call(bf16[8,512,256]{2,1,0:T(8,128)(2,1)} %bitcast.18, f32[8,16,64]{2,1,0:T(8,128)} %bitcast.21, f32[512,256]{1,0:T(8,128)} %get-tuple-element.20.grad_self, f32[16,64]{1,0:T(8,128)} %select_reduce_fusion.position_scores), custom_call_target="tpu_custom_call" | custom-call | tf_op jit(solution)/shard_map/scatter_rows/pallas_call | solution.py:273
  125.0 1.3 %copy.21 = f32[16,64]{1,0:T(8,128)} copy(f32[16,64]{1,0:T(8,128)} %get-tuple-element.27) | data formatting | bytes 8192
  126.3 1.9 %copy.22 = f32[512,256]{1,0:T(8,128)} copy(f32[512,256]{1,0:T(8,128)} %get-tuple-element.28) | data formatting | bytes 1048576
Async XLA Ops:
  85.7 7.4 %copy-start = (f32[64,128]{1,0:T(8,128)S(1)}, f32[64,128]{1,0:T(8,128)}, u32[]{:S(2)}) copy-start(f32[64,128]{1,0:T(8,128)} %param.27) | copy-start | bytes 98308
  85.7 7.4 %copy-start.2 = (f32[128]{0:T(128)S(1)}, f32[128]{0:T(128)}, u32[]{:S(2)}) copy-start(f32[128]{0:T(128)} %param.28) | copy-start | bytes 1540
  85.7 7.5 %copy-start.1 = (s32[16,64]{1,0:T(8,128)S(1)}, s32[16,64]{1,0:T(8,128)}, u32[]{:S(2)}) copy-start(s32[16,64]{1,0:T(8,128)} %param.26) | copy-start | bytes 12292

commit v5 on v4

--- a/solution.py
+++ b/solution.py
@@ -213,7 +213,7 @@
 
 
 def scatter_kernel(
-    chips, scale, parts, raw, grad_self, position_scores, grads, scores,
+    chips, scale, parts, raw, grad_self, positions, table, tower, grads, scores,
     near, sums, far, near_raw, sums_raw, far_raw, send, recv,
 ):
     me, core, ahead, behind = row_places(chips)
@@ -229,14 +229,9 @@
                 mine.at[ahead[i] * 2 + 1 - core], inbox.at[i],
                 send.at[n, i], recv.at[n, i], sibling,
             )
+            first[n, i].start()
+    second = []
     for i in order:
-        first[1, i].start()
-    first[0, order[0]].start()
-    second = []
-    for turn, i in enumerate(order):
-        first[0, i].wait_send()
-        if turn + 1 < chips:
-            first[0, order[turn + 1]].start()
         for n, (mine, inbox, summed, outbox) in enumerate(arrays):
             first[n, i].wait_recv()
             value = mine[ahead[i] * 2 + core].astype(f32) + inbox[i].astype(f32)
@@ -253,20 +248,29 @@
                 )
                 copy.start()
                 second.append((n, i, copy))
+    tower_values = jnp.sum(
+        jnp.maximum(table[...], 0.0) * tower[...], axis=-1, keepdims=True
+    )
+    places = positions[...]
+    position_scores = jnp.zeros(places.shape, f32)
+    for place in range(tower_values.shape[0]):
+        position_scores += jnp.where(
+            places == place, tower_values[place : place + 1, :], 0.0
+        )
     for n, i, copy in second:
         copy.wait_recv()
         if n == 0:
             grads[...] += far[i].astype(f32)
         else:
             scores[...] += far_raw[i]
-    scores[...] = scores[...] * scale + position_scores[...]
-    for i in order:
-        first[1, i].wait_send()
+    scores[...] = scores[...] * scale + position_scores
+    for copy in first.values():
+        copy.wait_send()
     for _, _, copy in second:
         copy.wait_send()
 
 
-def scatter_rows(row_count, parts, raw, grad_self, position_scores, scale):
+def scatter_rows(row_count, parts, raw, grad_self, positions, table, tower, scale):
     chips = row_count // 2
     part = parts.shape[1:]
     part_raw = raw.shape[1:]
@@ -274,9 +278,9 @@
         functools.partial(scatter_kernel, chips, scale),
         out_shape=(
             jax.ShapeDtypeStruct(grad_self.shape, f32),
-            jax.ShapeDtypeStruct(position_scores.shape, f32),
+            jax.ShapeDtypeStruct(positions.shape, f32),
         ),
-        in_specs=[pl.BlockSpec(memory_space=pltpu.VMEM)] * 4,
+        in_specs=[pl.BlockSpec(memory_space=pltpu.VMEM)] * 6,
         out_specs=(pl.BlockSpec(memory_space=pltpu.VMEM),) * 2,
         scratch_shapes=[pltpu.VMEM((chips,) + part, bf16)] * 3
         + [pltpu.VMEM((chips,) + part_raw, f32)] * 3
@@ -288,7 +292,7 @@
             collective_id=1, has_side_effects=True, vmem_limit_bytes=VMEM_LIMIT
         ),
         name="scatter_rows",
-    )(parts, raw, grad_self, position_scores)
+    )(parts, raw, grad_self, positions, table, tower[None])
 
 
 def node_kernel(
@@ -536,10 +540,6 @@
     column_items, packed = gather_rows(
         row_count, item_features, queries, candidates, score_cotangent
     )
-    tower_values = jnp.sum(jax.nn.relu(position_table) * tower_weight, axis=-1)
-    position_hits = positions[..., None] == jnp.arange(tower_values.shape[0])
-    position_scores = jnp.sum(jnp.where(position_hits, tower_values, 0.0), axis=-1)
-
     (parts,) = block_products(
         tiles, block_rows[0, 0], block_cols[0, 0], counts[0],
         column_items, col_count * rows_dev // block, False,
@@ -557,7 +557,9 @@
         back_parts.reshape(row_count, rows_dev, width),
         raw.reshape(row_count, -1, cands),
         grad_self,
-        position_scores,
+        positions,
+        position_table,
+        tower_weight,
         width ** (-0.5),
     )
     return (hidden, scores, item_grads)

time: 129 us -> 129 us (level)
    pallas_call x1, Pallas kernels: 56.7 us -> 54.7 us  [node_step(): pl.pallas_call(functools.partial(node_kernel, cols, steps), out_shape=(ja...]
    unnamed x8 -> x2, local copies, waits for them, and re-layouts: 3.18 us -> 3.16 us
where the time goes in v5:
time: 129 us; the launch traced here: 127 us
  Pallas kernels  123 us (95%)
  local copies, waits for them, and re-layouts  3.16 us (2%)
  between operations  1.32 us (1%)
    pallas_call x1, Pallas kernels, node_step(): pl.pallas_call(functools.partial(node_kernel, cols, steps), out_shape=(ja...  54.7 us
    pallas_call x1, Pallas kernels, scatter_rows(): pl.pallas_call(functools.partial(scatter_kernel, chips, scale), out_shape...  32.1 us
    pallas_call x1, Pallas kernels, gather_rows(): pl.pallas_call(functools.partial(gather_kernel, chips), out_shape=(jax.Sh...  21.1 us
    pallas_call x2, Pallas kernels, block_products(): pl.pallas_call(functools.partial(block_kernel, transpose, chunk, min(8, c...  14.9 us
    unnamed x2, local copies, waits for them, and re-layouts  3.16 us

profile of v5, /device:TPU:0, one launch (start us, length us, event | category | flops | bytes accessed | tf_op | source)
XLA Modules:
  0.0 127.3 jit_solution(5639803932310858308)
XLA Ops:
  1.3 21.1 %gather_rows.1 = (bf16[8,512,256]{2,1,0:T(8,128)(2,1)}, f32[8,16,384]{2,1,0:T(8,128)}) custom-call(bf16[512,256]{1,0:T(8,128)(2,1)} %items.3, bf16[16,256]{1,0:T(8,128)(2,1)} %queries.1, s32[16,64]{1,0:T(8,128)} %candidates.1, bf16[16,64]{1,0:T(8,128)(2,1)} %cotangent.1), custom_call_target="tpu_custom_call" | custom-call | tf_op jit(solution)/shard_map/gather_rows/pallas_call | solution.py:194
  22.4 7.1 %block_products.2 = bf16[16,128,256]{2,1,0:T(8,128)(2,1)} custom-call(s32[256]{0:T(256)} %bitcast.25, s32[256]{0:T(256)} %bitcast.23, s32[1]{0:T(128)} %bitcast.13.count, bf16[256,128,128]{2,1,0:T(8,128)(2,1)} %bitcast.15, bf16[32,128,256]{2,1,0:T(8,128)(2,1)} %bitcast.18), custom_call_target="tpu_custom_call" | custom-call | tf_op jit(solution)/shard_map/block_products/pallas_call | solution.py:76
  29.5 54.7 %node_step.1 = (bf16[512,256]{1,0:T(8,128)(2,1)}, f32[512,256]{1,0:T(8,128)}, bf16[4,512,256]{2,1,0:T(8,128)(2,1)}, f32[128,64]{1,0:T(8,128)}) custom-call(bf16[512,256]{1,0:T(8,128)(2,1)} %items.3, bf16[4,512,256]{2,1,0:T(8,128)(2,1)} %bitcast.17, bf16[256,256]{1,0:T(8,128)(2,1)} %w_self.1, bf16[256,256]{1,0:T(8,128)(2,1)} %w_neighbor.1, ...), custom_call_target="tpu_custom_call" | custom-call | tf_op jit(solution)/shard_map/node_step/pallas_call | solution.py:483
  84.2 7.9 %block_products.3 = (bf16[32,128,256]{2,1,0:T(8,128)(2,1)}, bf16[512,256]{1,0:T(8,128)(2,1)}) custom-call(s32[256]{0:T(256)} %bitcast.24, s32[256]{0:T(256)} %bitcast.26, s32[1]{0:T(128)} %bitcast.14.count, bf16[256,128,128]{2,1,0:T(8,128)(2,1)} %bitcast.16, bf16[16,128,256]{2,1,0:T(8,128)(2,1)} %bitcast.20, bf16[512,256]{1,0:T(8,128)(2,1)} %get-tuple-element.16.refs_0_), custom_call_target="tpu_custom_call" | custom-call | tf_op jit(solution)/shard_map/block_products/pallas_call | solution.py:76
  92.0 32.1 %scatter_rows.1 = (f32[512,256]{1,0:T(8,128)}, f32[16,64]{1,0:T(8,128)}) custom-call(bf16[8,512,256]{2,1,0:T(8,128)(2,1)} %bitcast.19, f32[8,16,64]{2,1,0:T(8,128)} %bitcast.22, f32[512,256]{1,0:T(8,128)} %get-tuple-element.20.grad_self, s32[16,64]{1,0:T(8,128)} %positions.1, f32[64,128]{1,0:T(8,128)} %table.1, f32[1,128]{1,0:T(1,128)} %bitcast.29), custom_call_target="tpu_custom_call" | custom-call | tf_op jit(solution)/shard_map/scatter_rows/pallas_call | solution.py:277
  124.1 1.3 %copy.21 = f32[16,64]{1,0:T(8,128)} copy(f32[16,64]{1,0:T(8,128)} %get-tuple-element.27) | data formatting | bytes 8192
  125.4 1.9 %copy.22 = f32[512,256]{1,0:T(8,128)} copy(f32[512,256]{1,0:T(8,128)} %get-tuple-element.28) | data formatting | bytes 1048576
